TPU v7x, 128 devices: a whole 4x4x4 slice. The times are simulated.
128 devices in a mesh: ctx: 32 (over x, y, z_hi), mem: 4 (over z_lo, core).
Axes of the slice: x: 4, y: 4, z: 4 (z_hi: 2, z_lo: 2; z = z_hi * 2 + z_lo), core: 2. Of those that a mesh axis runs over, the one named last changes fastest.
Arguments:
- queries: bfloat16 [8192, 4096], P('ctx', 'mem')
- keys: bfloat16 [8192, 1024], P('ctx', 'mem')
- values: bfloat16 [8192, 1024], P('ctx', 'mem'), may hold values from -6 to 6
- mem_keys: bfloat16 [1024, 64, 1024], P('ctx', None, 'mem')
- mem_values: bfloat16 [1024, 64, 1024], P('ctx', None, 'mem'), may hold values from -6 to 6
- retrieval: int32 [64, 4, 32], P('ctx', 'mem'), may hold values from 0 to 1023, as said below
- gate_weight: bfloat16 [2, 4096, 32], P(None, 'mem'), may hold values from -0.375 to 0.375
- gate_bias: float32 [32], P('mem'), may hold values from -2 to 2
Outputs:
- mixed: bfloat16 [8192, 4096], P('ctx', 'mem')
Inputs may be any that keep to these rules, and one draw needn't show every extreme that they name: Each list retrieval[b, g] names 32 distinct blocks. At most 2 of them lie in one shard of 32 consecutive blocks; one shard, the same for all lists, holds exactly 2 blocks of every list.
All inputs are finite; a program needn't handle non-finite values.
Results may differ from a plain program's by a relative error of at most 0.013.
Values may be sent and summed in bfloat16 or wider, within the bound.
A program may use at most 192 MiB of HBM per device.

v0:
```python
from functools import partial

import jax
import jax.numpy as jnp
from jax import lax
from jax.sharding import PartitionSpec as P

QBLK = 128
TOPB = 32


def passed_along(x, axis, by):
    peers = lax.axis_size(axis)
    pairs = [(i, i + by) for i in range(peers) if 0 <= i + by < peers]
    return lax.ppermute(x, axis, pairs)


def tile_update(state, q_rows, piece, start, q_pos, scale):
    best, total, acc = state
    count = piece.shape[1]
    kv_heads = q_rows.shape[1]
    head_dim = q_rows.shape[3]
    k_rows = piece[0].reshape(count, kv_heads, head_dim)
    v_rows = piece[1].reshape(count, kv_heads, head_dim)
    scores = (
        jnp.einsum("qkgd,skd->kgqs", q_rows, k_rows, preferred_element_type=jnp.float32) * scale
    )
    k_pos = start + jnp.arange(count, dtype=jnp.int32)
    visible = (k_pos // QBLK)[None, :] <= (q_pos // QBLK)[:, None]
    scores = jnp.where(visible[None, None], scores, -jnp.inf)
    newest = jnp.maximum(best, jnp.max(scores, axis=3))
    factor = jnp.exp(best - newest)
    weights = jnp.exp(scores - newest[..., None])
    total = total * factor + jnp.sum(weights, axis=3)
    update = jnp.einsum(
        "kgqs,skd->kgqd", weights.astype(jnp.bfloat16), v_rows, preferred_element_type=jnp.float32
    )
    acc = acc * factor[..., None] + update
    return (newest, total, acc)


def memory_attend(operands, scale):
    q_block, block_keys, block_vals = operands
    scores = (
        jnp.einsum("qkgd,skd->kgqs", q_block, block_keys, preferred_element_type=jnp.float32)
        * scale
    )
    top = jnp.max(scores, axis=3, keepdims=True)
    weights = jnp.exp(scores - top)
    total = jnp.sum(weights, axis=3, keepdims=True)
    result = (
        jnp.einsum(
            "kgqs,skd->kgqd",
            weights.astype(jnp.bfloat16),
            block_vals,
            preferred_element_type=jnp.float32,
        )
        / total
    )
    return result.transpose(2, 0, 1, 3).reshape(q_block.shape[0], -1)


def on_device(queries, keys, values, mem_keys, mem_values, retrieval, gate_weight, gate_bias):
    cycle = lax.axis_size("ctx")
    place = lax.axis_index("ctx")
    rows, width = queries.shape
    heads = gate_bias.shape[0]
    head_dim = width // heads
    kv_width = keys.shape[1]
    kv_heads = kv_width // head_dim
    share_count = heads // kv_heads
    scale = head_dim ** (-0.5)
    q_rows = queries.reshape(rows, kv_heads, share_count, head_dim)
    q_pos = place * rows + jnp.arange(rows, dtype=jnp.int32)
    stacked = jnp.stack([keys, values])
    start_state = (
        jnp.full((kv_heads, share_count, rows), -1e30, jnp.float32),
        jnp.zeros((kv_heads, share_count, rows), jnp.float32),
        jnp.zeros((kv_heads, share_count, rows, head_dim), jnp.float32),
    )
    state = tile_update(start_state, q_rows, stacked, place * rows, q_pos, scale)

    def cycle_step(turn, carry):
        held, inner = carry
        held = passed_along(held, "ctx", 1)
        source = (place - turn) % cycle
        inner = tile_update(inner, q_rows, held, source * rows, q_pos, scale)
        return (held, inner)

    _, state = lax.fori_loop(1, cycle, cycle_step, (stacked, state))
    local = state[2] / state[1][..., None]
    local_tok = local.transpose(2, 0, 1, 3).reshape(rows, width)
    lists = retrieval.reshape(-1, TOPB)
    blocks_dev = lists.shape[0]
    shard_blocks = mem_keys.shape[0]
    cap = max(2, 2 * TOPB // cycle)
    slots = blocks_dev * cap
    owner = lists // shard_blocks
    offset = lists % shard_blocks
    order = jnp.arange(TOPB, dtype=jnp.int32)
    earlier = order[None, :] < order[:, None]
    same_owner = owner[:, :, None] == owner[:, None, :]
    rank = jnp.sum(jnp.logical_and(same_owner, earlier[None]), axis=2)
    slot = jnp.arange(blocks_dev, dtype=jnp.int32)[:, None] * cap + rank
    request = (
        jnp.full((cycle, slots), -1, jnp.int32)
        .at[owner.reshape(-1), slot.reshape(-1)]
        .set(offset.reshape(-1))
    )
    asked = lax.all_to_all(request, "ctx", split_axis=0, concat_axis=0, tiled=True)
    valid = (asked >= 0).reshape(-1)[:, None, None]
    wanted = jnp.maximum(asked, 0).reshape(-1)
    send_keys = jnp.where(valid, jnp.take(mem_keys, wanted, axis=0), 0)
    send_vals = jnp.where(valid, jnp.take(mem_values, wanted, axis=0), 0)
    block_rows = mem_keys.shape[1]
    send_keys = send_keys.reshape(cycle, slots, block_rows, kv_width)
    send_vals = send_vals.reshape(cycle, slots, block_rows, kv_width)
    got_keys, got_vals = (
        lax.all_to_all(send_keys, "ctx", split_axis=0, concat_axis=0, tiled=True),
        lax.all_to_all(send_vals, "ctx", split_axis=0, concat_axis=0, tiled=True),
    )
    where_from = (owner * slots + slot).reshape(-1)
    fetched_keys = jnp.take(
        got_keys.reshape(cycle * slots, block_rows, kv_width), where_from, axis=0
    )
    fetched_vals = jnp.take(
        got_vals.reshape(cycle * slots, block_rows, kv_width), where_from, axis=0
    )
    fetched_keys = fetched_keys.reshape(blocks_dev, TOPB * block_rows, kv_heads, head_dim)
    fetched_vals = fetched_vals.reshape(blocks_dev, TOPB * block_rows, kv_heads, head_dim)
    q_blocks = queries.reshape(blocks_dev, QBLK, kv_heads, share_count, head_dim)
    memory = lax.map(partial(memory_attend, scale=scale), (q_blocks, fetched_keys, fetched_vals))
    memory_tok = memory.reshape(rows, width)
    partial_logits = jnp.dot(
        local_tok.astype(jnp.bfloat16), gate_weight[0], preferred_element_type=jnp.float32
    )
    partial_logits = partial_logits + jnp.dot(
        memory_tok.astype(jnp.bfloat16), gate_weight[1], preferred_element_type=jnp.float32
    )
    all_logits = lax.psum(partial_logits.astype(jnp.bfloat16), "mem").astype(jnp.float32)
    group = lax.axis_index("mem")
    logits = lax.dynamic_slice_in_dim(all_logits, group * heads, heads, 1)
    logits = logits + gate_bias[None, :]
    share = jax.nn.sigmoid(logits)[:, :, None]
    mixed = share * memory_tok.reshape(rows, heads, head_dim) + (1.0 - share) * local_tok.reshape(
        rows, heads, head_dim
    )
    return mixed.reshape(rows, width).astype(jnp.bfloat16)


def solution(mesh):
    placed = (
        P("ctx", "mem"),
        P("ctx", "mem"),
        P("ctx", "mem"),
        P("ctx", None, "mem"),
        P("ctx", None, "mem"),
        P("ctx", "mem", None),
        P(None, "mem", None),
        P("mem"),
    )
    return jax.shard_map(
        on_device, mesh=mesh, in_specs=placed, out_specs=P("ctx", "mem"), check_vma=False
    )
```

profile of v0, /device:TPU:2, one launch (start us, length us, event | category | flops | bytes accessed | tf_op | source)
XLA Modules:
  0.0 686.0 jit_solution(9450929592874255486)
XLA Ops:
  3.9 3.5 scatter_fusion
  7.5 19.3 %all_to_all.19 = s32[32,1,4]{2,1,0:T(1,128)S(1)} all-to-all(s32[32,1,4]{2,1,0:T(1,128)S(1)} %copy.78), channel_id=1, replica_groups=mesh['ctx'=32,'mem'=4] {'ctx'}, dimensions={0} | all-to-all | bytes 1024 | tf_op jit(solution)/shard_map/all_to_all | solution.py:110
  32.7 6.3 select_select_fusion
  39.1 6.0 all-to-all-start.1
  49.1 48.6 %all-to-all-done.1 = bf16[32,4,64,256]{3,2,1,0:T(8,128)(2,1)} async-done(((bf16[32,4,64,256]{3,2,1,0:T(8,128)(2,1)}), bf16[32,4,64,256]{3,2,1,0:T(8,128)(2,1)}, u32[]{:S(2)}, u32[]{:S(2)}) %all-to-all-start.1) | async-done | bytes 4194336 | tf_op jit(solution)/shard_map/all_to_all | solution.py:119
  97.7 6.7 all-to-all-start.2
  104.4 516.6 %while.35 = (s32[]{:T(128)}, bf16[2,256,256]{1,2,0:T(8,128)(2,1)S(1)}, f32[2,4,256]{2,1,0:T(4,128)S(1)}, f32[2,4,256]{2,1,0:T(4,128)S(1)}, f32[2,4,256,128]{3,2,...) while((s32[]{:T(128)}, ...), condition=%wide.region_5.6_spmd.clone.clone, body=%wide.region_2.5_spmd.clone.clone.sunk | while | flops 272708096 | bytes 11541306 | solution.py:90
  104.4 4.9 collective-permute-start
  109.4 54.1 %collective-permute-done = bf16[2,256,256]{1,2,0:T(8,128)(2,1)S(1)} collective-permute-done((bf16[2,256,256]{1,2,0:T(8,128)(2,1)S(1)}, bf16[2,256,256]{1,2,0:T(8,128)(2,1)S(1)}, u32[]{:S(2)}, u32[]{:S(2)}) %collective-permute-start) | collective-permute-done | bytes 262176 | tf_op jit(solution)/shard_map/while/body/eval_jaxpr/ppermute | solution.py:15
  167.6 10.7 %collective-permute-done = bf16[2,256,256]{1,2,0:T(8,128)(2,1)S(1)} collective-permute-done((bf16[2,256,256]{1,2,0:T(8,128)(2,1)S(1)}, bf16[2,256,256]{1,2,0:T(8,128)(2,1)S(1)}, u32[]{:S(2)}, u32[]{:S(2)}) %collective-permute-start) | collective-permute-done | bytes 262176 | tf_op jit(solution)/shard_map/while/body/eval_jaxpr/ppermute | solution.py:15
  182.3 10.7 %collective-permute-done = bf16[2,256,256]{1,2,0:T(8,128)(2,1)S(1)} collective-permute-done((bf16[2,256,256]{1,2,0:T(8,128)(2,1)S(1)}, bf16[2,256,256]{1,2,0:T(8,128)(2,1)S(1)}, u32[]{:S(2)}, u32[]{:S(2)}) %collective-permute-start) | collective-permute-done | bytes 262176 | tf_op jit(solution)/shard_map/while/body/eval_jaxpr/ppermute | solution.py:15
  196.9 10.7 %collective-permute-done = bf16[2,256,256]{1,2,0:T(8,128)(2,1)S(1)} collective-permute-done((bf16[2,256,256]{1,2,0:T(8,128)(2,1)S(1)}, bf16[2,256,256]{1,2,0:T(8,128)(2,1)S(1)}, u32[]{:S(2)}, u32[]{:S(2)}) %collective-permute-start) | collective-permute-done | bytes 262176 | tf_op jit(solution)/shard_map/while/body/eval_jaxpr/ppermute | solution.py:15
  211.6 10.7 %collective-permute-done = bf16[2,256,256]{1,2,0:T(8,128)(2,1)S(1)} collective-permute-done((bf16[2,256,256]{1,2,0:T(8,128)(2,1)S(1)}, bf16[2,256,256]{1,2,0:T(8,128)(2,1)S(1)}, u32[]{:S(2)}, u32[]{:S(2)}) %collective-permute-start) | collective-permute-done | bytes 262176 | tf_op jit(solution)/shard_map/while/body/eval_jaxpr/ppermute | solution.py:15
  226.3 10.7 %collective-permute-done = bf16[2,256,256]{1,2,0:T(8,128)(2,1)S(1)} collective-permute-done((bf16[2,256,256]{1,2,0:T(8,128)(2,1)S(1)}, bf16[2,256,256]{1,2,0:T(8,128)(2,1)S(1)}, u32[]{:S(2)}, u32[]{:S(2)}) %collective-permute-start) | collective-permute-done | bytes 262176 | tf_op jit(solution)/shard_map/while/body/eval_jaxpr/ppermute | solution.py:15
  241.0 10.7 %collective-permute-done = bf16[2,256,256]{1,2,0:T(8,128)(2,1)S(1)} collective-permute-done((bf16[2,256,256]{1,2,0:T(8,128)(2,1)S(1)}, bf16[2,256,256]{1,2,0:T(8,128)(2,1)S(1)}, u32[]{:S(2)}, u32[]{:S(2)}) %collective-permute-start) | collective-permute-done | bytes 262176 | tf_op jit(solution)/shard_map/while/body/eval_jaxpr/ppermute | solution.py:15
  255.7 11.4 %collective-permute-done = bf16[2,256,256]{1,2,0:T(8,128)(2,1)S(1)} collective-permute-done((bf16[2,256,256]{1,2,0:T(8,128)(2,1)S(1)}, bf16[2,256,256]{1,2,0:T(8,128)(2,1)S(1)}, u32[]{:S(2)}, u32[]{:S(2)}) %collective-permute-start) | collective-permute-done | bytes 262176 | tf_op jit(solution)/shard_map/while/body/eval_jaxpr/ppermute | solution.py:15
  271.0 12.5 %collective-permute-done = bf16[2,256,256]{1,2,0:T(8,128)(2,1)S(1)} collective-permute-done((bf16[2,256,256]{1,2,0:T(8,128)(2,1)S(1)}, bf16[2,256,256]{1,2,0:T(8,128)(2,1)S(1)}, u32[]{:S(2)}, u32[]{:S(2)}) %collective-permute-start) | collective-permute-done | bytes 262176 | tf_op jit(solution)/shard_map/while/body/eval_jaxpr/ppermute | solution.py:15
  287.6 13.3 %collective-permute-done = bf16[2,256,256]{1,2,0:T(8,128)(2,1)S(1)} collective-permute-done((bf16[2,256,256]{1,2,0:T(8,128)(2,1)S(1)}, bf16[2,256,256]{1,2,0:T(8,128)(2,1)S(1)}, u32[]{:S(2)}, u32[]{:S(2)}) %collective-permute-start) | collective-permute-done | bytes 262176 | tf_op jit(solution)/shard_map/while/body/eval_jaxpr/ppermute | solution.py:15
  304.9 12.4 %collective-permute-done = bf16[2,256,256]{1,2,0:T(8,128)(2,1)S(1)} collective-permute-done((bf16[2,256,256]{1,2,0:T(8,128)(2,1)S(1)}, bf16[2,256,256]{1,2,0:T(8,128)(2,1)S(1)}, u32[]{:S(2)}, u32[]{:S(2)}) %collective-permute-start) | collective-permute-done | bytes 262176 | tf_op jit(solution)/shard_map/while/body/eval_jaxpr/ppermute | solution.py:15
  321.3 11.5 %collective-permute-done = bf16[2,256,256]{1,2,0:T(8,128)(2,1)S(1)} collective-permute-done((bf16[2,256,256]{1,2,0:T(8,128)(2,1)S(1)}, bf16[2,256,256]{1,2,0:T(8,128)(2,1)S(1)}, u32[]{:S(2)}, u32[]{:S(2)}) %collective-permute-start) | collective-permute-done | bytes 262176 | tf_op jit(solution)/shard_map/while/body/eval_jaxpr/ppermute | solution.py:15
  336.9 10.7 %collective-permute-done = bf16[2,256,256]{1,2,0:T(8,128)(2,1)S(1)} collective-permute-done((bf16[2,256,256]{1,2,0:T(8,128)(2,1)S(1)}, bf16[2,256,256]{1,2,0:T(8,128)(2,1)S(1)}, u32[]{:S(2)}, u32[]{:S(2)}) %collective-permute-start) | collective-permute-done | bytes 262176 | tf_op jit(solution)/shard_map/while/body/eval_jaxpr/ppermute | solution.py:15
  351.6 10.7 %collective-permute-done = bf16[2,256,256]{1,2,0:T(8,128)(2,1)S(1)} collective-permute-done((bf16[2,256,256]{1,2,0:T(8,128)(2,1)S(1)}, bf16[2,256,256]{1,2,0:T(8,128)(2,1)S(1)}, u32[]{:S(2)}, u32[]{:S(2)}) %collective-permute-start) | collective-permute-done | bytes 262176 | tf_op jit(solution)/shard_map/while/body/eval_jaxpr/ppermute | solution.py:15
  366.2 10.7 %collective-permute-done = bf16[2,256,256]{1,2,0:T(8,128)(2,1)S(1)} collective-permute-done((bf16[2,256,256]{1,2,0:T(8,128)(2,1)S(1)}, bf16[2,256,256]{1,2,0:T(8,128)(2,1)S(1)}, u32[]{:S(2)}, u32[]{:S(2)}) %collective-permute-start) | collective-permute-done | bytes 262176 | tf_op jit(solution)/shard_map/while/body/eval_jaxpr/ppermute | solution.py:15
  380.9 10.7 %collective-permute-done = bf16[2,256,256]{1,2,0:T(8,128)(2,1)S(1)} collective-permute-done((bf16[2,256,256]{1,2,0:T(8,128)(2,1)S(1)}, bf16[2,256,256]{1,2,0:T(8,128)(2,1)S(1)}, u32[]{:S(2)}, u32[]{:S(2)}) %collective-permute-start) | collective-permute-done | bytes 262176 | tf_op jit(solution)/shard_map/while/body/eval_jaxpr/ppermute | solution.py:15
  395.6 10.7 %collective-permute-done = bf16[2,256,256]{1,2,0:T(8,128)(2,1)S(1)} collective-permute-done((bf16[2,256,256]{1,2,0:T(8,128)(2,1)S(1)}, bf16[2,256,256]{1,2,0:T(8,128)(2,1)S(1)}, u32[]{:S(2)}, u32[]{:S(2)}) %collective-permute-start) | collective-permute-done | bytes 262176 | tf_op jit(solution)/shard_map/while/body/eval_jaxpr/ppermute | solution.py:15
  410.3 10.7 %collective-permute-done = bf16[2,256,256]{1,2,0:T(8,128)(2,1)S(1)} collective-permute-done((bf16[2,256,256]{1,2,0:T(8,128)(2,1)S(1)}, bf16[2,256,256]{1,2,0:T(8,128)(2,1)S(1)}, u32[]{:S(2)}, u32[]{:S(2)}) %collective-permute-start) | collective-permute-done | bytes 262176 | tf_op jit(solution)/shard_map/while/body/eval_jaxpr/ppermute | solution.py:15
  425.0 10.7 %collective-permute-done = bf16[2,256,256]{1,2,0:T(8,128)(2,1)S(1)} collective-permute-done((bf16[2,256,256]{1,2,0:T(8,128)(2,1)S(1)}, bf16[2,256,256]{1,2,0:T(8,128)(2,1)S(1)}, u32[]{:S(2)}, u32[]{:S(2)}) %collective-permute-start) | collective-permute-done | bytes 262176 | tf_op jit(solution)/shard_map/while/body/eval_jaxpr/ppermute | solution.py:15
  439.6 10.7 %collective-permute-done = bf16[2,256,256]{1,2,0:T(8,128)(2,1)S(1)} collective-permute-done((bf16[2,256,256]{1,2,0:T(8,128)(2,1)S(1)}, bf16[2,256,256]{1,2,0:T(8,128)(2,1)S(1)}, u32[]{:S(2)}, u32[]{:S(2)}) %collective-permute-start) | collective-permute-done | bytes 262176 | tf_op jit(solution)/shard_map/while/body/eval_jaxpr/ppermute | solution.py:15
  454.4 11.8 %collective-permute-done = bf16[2,256,256]{1,2,0:T(8,128)(2,1)S(1)} collective-permute-done((bf16[2,256,256]{1,2,0:T(8,128)(2,1)S(1)}, bf16[2,256,256]{1,2,0:T(8,128)(2,1)S(1)}, u32[]{:S(2)}, u32[]{:S(2)}) %collective-permute-start) | collective-permute-done | bytes 262176 | tf_op jit(solution)/shard_map/while/body/eval_jaxpr/ppermute | solution.py:15
  470.3 13.1 %collective-permute-done = bf16[2,256,256]{1,2,0:T(8,128)(2,1)S(1)} collective-permute-done((bf16[2,256,256]{1,2,0:T(8,128)(2,1)S(1)}, bf16[2,256,256]{1,2,0:T(8,128)(2,1)S(1)}, u32[]{:S(2)}, u32[]{:S(2)}) %collective-permute-start) | collective-permute-done | bytes 262176 | tf_op jit(solution)/shard_map/while/body/eval_jaxpr/ppermute | solution.py:15
  487.3 12.7 %collective-permute-done = bf16[2,256,256]{1,2,0:T(8,128)(2,1)S(1)} collective-permute-done((bf16[2,256,256]{1,2,0:T(8,128)(2,1)S(1)}, bf16[2,256,256]{1,2,0:T(8,128)(2,1)S(1)}, u32[]{:S(2)}, u32[]{:S(2)}) %collective-permute-start) | collective-permute-done | bytes 262176 | tf_op jit(solution)/shard_map/while/body/eval_jaxpr/ppermute | solution.py:15
  504.1 11.9 %collective-permute-done = bf16[2,256,256]{1,2,0:T(8,128)(2,1)S(1)} collective-permute-done((bf16[2,256,256]{1,2,0:T(8,128)(2,1)S(1)}, bf16[2,256,256]{1,2,0:T(8,128)(2,1)S(1)}, u32[]{:S(2)}, u32[]{:S(2)}) %collective-permute-start) | collective-permute-done | bytes 262176 | tf_op jit(solution)/shard_map/while/body/eval_jaxpr/ppermute | solution.py:15
  520.0 11.0 %collective-permute-done = bf16[2,256,256]{1,2,0:T(8,128)(2,1)S(1)} collective-permute-done((bf16[2,256,256]{1,2,0:T(8,128)(2,1)S(1)}, bf16[2,256,256]{1,2,0:T(8,128)(2,1)S(1)}, u32[]{:S(2)}, u32[]{:S(2)}) %collective-permute-start) | collective-permute-done | bytes 262176 | tf_op jit(solution)/shard_map/while/body/eval_jaxpr/ppermute | solution.py:15
  535.0 10.7 %collective-permute-done = bf16[2,256,256]{1,2,0:T(8,128)(2,1)S(1)} collective-permute-done((bf16[2,256,256]{1,2,0:T(8,128)(2,1)S(1)}, bf16[2,256,256]{1,2,0:T(8,128)(2,1)S(1)}, u32[]{:S(2)}, u32[]{:S(2)}) %collective-permute-start) | collective-permute-done | bytes 262176 | tf_op jit(solution)/shard_map/while/body/eval_jaxpr/ppermute | solution.py:15
  549.7 10.7 %collective-permute-done = bf16[2,256,256]{1,2,0:T(8,128)(2,1)S(1)} collective-permute-done((bf16[2,256,256]{1,2,0:T(8,128)(2,1)S(1)}, bf16[2,256,256]{1,2,0:T(8,128)(2,1)S(1)}, u32[]{:S(2)}, u32[]{:S(2)}) %collective-permute-start) | collective-permute-done | bytes 262176 | tf_op jit(solution)/shard_map/while/body/eval_jaxpr/ppermute | solution.py:15
  564.4 10.7 %collective-permute-done = bf16[2,256,256]{1,2,0:T(8,128)(2,1)S(1)} collective-permute-done((bf16[2,256,256]{1,2,0:T(8,128)(2,1)S(1)}, bf16[2,256,256]{1,2,0:T(8,128)(2,1)S(1)}, u32[]{:S(2)}, u32[]{:S(2)}) %collective-permute-start) | collective-permute-done | bytes 262176 | tf_op jit(solution)/shard_map/while/body/eval_jaxpr/ppermute | solution.py:15
  579.1 10.7 %collective-permute-done = bf16[2,256,256]{1,2,0:T(8,128)(2,1)S(1)} collective-permute-done((bf16[2,256,256]{1,2,0:T(8,128)(2,1)S(1)}, bf16[2,256,256]{1,2,0:T(8,128)(2,1)S(1)}, u32[]{:S(2)}, u32[]{:S(2)}) %collective-permute-start) | collective-permute-done | bytes 262176 | tf_op jit(solution)/shard_map/while/body/eval_jaxpr/ppermute | solution.py:15
  593.8 10.7 %collective-permute-done = bf16[2,256,256]{1,2,0:T(8,128)(2,1)S(1)} collective-permute-done((bf16[2,256,256]{1,2,0:T(8,128)(2,1)S(1)}, bf16[2,256,256]{1,2,0:T(8,128)(2,1)S(1)}, u32[]{:S(2)}, u32[]{:S(2)}) %collective-permute-start) | collective-permute-done | bytes 262176 | tf_op jit(solution)/shard_map/while/body/eval_jaxpr/ppermute | solution.py:15
  608.4 10.7 %collective-permute-done = bf16[2,256,256]{1,2,0:T(8,128)(2,1)S(1)} collective-permute-done((bf16[2,256,256]{1,2,0:T(8,128)(2,1)S(1)}, bf16[2,256,256]{1,2,0:T(8,128)(2,1)S(1)}, u32[]{:S(2)}, u32[]{:S(2)}) %collective-permute-start) | collective-permute-done | bytes 262176 | tf_op jit(solution)/shard_map/while/body/eval_jaxpr/ppermute | solution.py:15
  626.6 4.2 gather_fusion.3
  630.7 4.0 broadcast_select_fusion
  637.2 4.0 reshape.419
  641.3 30.3 %while.34 = (s32[]{:T(128)}, f32[2,128,1024]{2,1,0:T(8,128)}, bf16[2,2048,2,128]{3,2,1,0:T(2,128)(2,1)S(1)}, bf16[2,128,2,4,128]{4,3,2,1,0:T(4,128)(2,1)}, bf16[2,2048,2,128]{3,2,1,0:T(2,128)(2,1)}, /*index=5*/s32[]{:T(128)}) while((s32[]{:T(128)}, f32[2,128,1024]{2,1,0:T(8,128)}, bf16[2,2048,2,128]{3,2,1,0:T(2,128)(2,1)S(1)}, ...), condition=%wide.region_11.14_spmd, body=%wide.region_8.13_spmd.sunk | while | flops 1090648064 | bytes 89412288 | solution.py:132
  641.3 3.0 constant_dynamic-slice_fusion.6
  649.7 4.9 fusion.71
  656.4 3.0 constant_dynamic-slice_fusion.6
  664.8 4.9 fusion.71
  673.4 10.3 %psum.7 = bf16[256,32]{0,1:T(8,128)(2,1)S(1)} all-reduce(bf16[256,32]{0,1:T(8,128)(2,1)S(1)} %fusion.31), channel_id=1, replica_groups=mesh['ctx'=32,'mem'=4] {'mem'}, use_global_device_ids=true, to_apply=%region_12.15 | all-reduce | flops 8192 | bytes 32768 | tf_op jit(solution)/shard_map/psum | solution.py:140
  (509 shorter events, 159.8 us)
Async XLA Ops:
  0.0 27.0 %copy-start = (bf16[32,64,256]{2,1,0:T(8,128)(2,1)S(1)}, bf16[32,64,256]{2,1,0:T(8,128)(2,1)}, u32[]{:S(2)}) copy-start(bf16[32,64,256]{2,1,0:T(8,128)(2,1)} %param.19) | copy-start | bytes 3145732
  27.0 2.8 copy-start.5
  39.1 6.1 copy-start.10
  39.1 58.6 %all-to-all-start.1 = ((bf16[32,4,64,256]{3,2,1,0:T(8,128)(2,1)}), bf16[32,4,64,256]{3,2,1,0:T(8,128)(2,1)}, u32[]{:S(2)}, u32[]{:S(2)}) async-start(bf16[32,4,64,256]{3,2,1,0:T(8,128)(2,1)} %bitcast.153), calls=%async_computation.1 | async-start | bytes 8388608 | tf_op jit(solution)/shard_map/all_to_all | solution.py:119
  97.7 528.9 %all-to-all-start.2 = ((bf16[32,4,64,256]{3,2,1,0:T(8,128)(2,1)}), bf16[32,4,64,256]{3,2,1,0:T(8,128)(2,1)}, u32[]{:S(2)}, u32[]{:S(2)}) async-start(bf16[32,4,64,256]{3,2,1,0:T(8,128)(2,1)} %bitcast.152), calls=%async_computation.2 | async-start | bytes 8388608 | tf_op jit(solution)/shard_map/all_to_all | solution.py:120
  104.4 59.2 %collective-permute-start = (bf16[2,256,256]{1,2,0:T(8,128)(2,1)S(1)}, bf16[2,256,256]{1,2,0:T(8,128)(2,1)S(1)}, u32[]{:S(2)}, u32[]{:S(2)}) collective-permute-start(bf16[2,256,256]{1,2,0:T(8,128)(2,1)S(1)} %get-tuple-element.548), channel_id=1, source_target_pairs={{0,4},{4,8},{8,12},{12,16},{16,20},{20,24},{24,28},{28,32},{32,36}... | collective-permute-start | bytes 786440 | tf_op jit(solution)/shard_map/while/body/eval_jaxpr/ppermute | solution.py:15
  165.5 12.8 %collective-permute-start = (bf16[2,256,256]{1,2,0:T(8,128)(2,1)S(1)}, bf16[2,256,256]{1,2,0:T(8,128)(2,1)S(1)}, u32[]{:S(2)}, u32[]{:S(2)}) collective-permute-start(bf16[2,256,256]{1,2,0:T(8,128)(2,1)S(1)} %get-tuple-element.548), channel_id=1, source_target_pairs={{0,4},{4,8},{8,12},{12,16},{16,20},{20,24},{24,28},{28,32},{32,36}... | collective-permute-start | bytes 786440 | tf_op jit(solution)/shard_map/while/body/eval_jaxpr/ppermute | solution.py:15
  180.1 12.8 %collective-permute-start = (bf16[2,256,256]{1,2,0:T(8,128)(2,1)S(1)}, bf16[2,256,256]{1,2,0:T(8,128)(2,1)S(1)}, u32[]{:S(2)}, u32[]{:S(2)}) collective-permute-start(bf16[2,256,256]{1,2,0:T(8,128)(2,1)S(1)} %get-tuple-element.548), channel_id=1, source_target_pairs={{0,4},{4,8},{8,12},{12,16},{16,20},{20,24},{24,28},{28,32},{32,36}... | collective-permute-start | bytes 786440 | tf_op jit(solution)/shard_map/while/body/eval_jaxpr/ppermute | solution.py:15
  194.8 12.8 %collective-permute-start = (bf16[2,256,256]{1,2,0:T(8,128)(2,1)S(1)}, bf16[2,256,256]{1,2,0:T(8,128)(2,1)S(1)}, u32[]{:S(2)}, u32[]{:S(2)}) collective-permute-start(bf16[2,256,256]{1,2,0:T(8,128)(2,1)S(1)} %get-tuple-element.548), channel_id=1, source_target_pairs={{0,4},{4,8},{8,12},{12,16},{16,20},{20,24},{24,28},{28,32},{32,36}... | collective-permute-start | bytes 786440 | tf_op jit(solution)/shard_map/while/body/eval_jaxpr/ppermute | solution.py:15
  209.5 12.8 %collective-permute-start = (bf16[2,256,256]{1,2,0:T(8,128)(2,1)S(1)}, bf16[2,256,256]{1,2,0:T(8,128)(2,1)S(1)}, u32[]{:S(2)}, u32[]{:S(2)}) collective-permute-start(bf16[2,256,256]{1,2,0:T(8,128)(2,1)S(1)} %get-tuple-element.548), channel_id=1, source_target_pairs={{0,4},{4,8},{8,12},{12,16},{16,20},{20,24},{24,28},{28,32},{32,36}... | collective-permute-start | bytes 786440 | tf_op jit(solution)/shard_map/while/body/eval_jaxpr/ppermute | solution.py:15
  224.2 12.8 %collective-permute-start = (bf16[2,256,256]{1,2,0:T(8,128)(2,1)S(1)}, bf16[2,256,256]{1,2,0:T(8,128)(2,1)S(1)}, u32[]{:S(2)}, u32[]{:S(2)}) collective-permute-start(bf16[2,256,256]{1,2,0:T(8,128)(2,1)S(1)} %get-tuple-element.548), channel_id=1, source_target_pairs={{0,4},{4,8},{8,12},{12,16},{16,20},{20,24},{24,28},{28,32},{32,36}... | collective-permute-start | bytes 786440 | tf_op jit(solution)/shard_map/while/body/eval_jaxpr/ppermute | solution.py:15
  238.9 12.8 %collective-permute-start = (bf16[2,256,256]{1,2,0:T(8,128)(2,1)S(1)}, bf16[2,256,256]{1,2,0:T(8,128)(2,1)S(1)}, u32[]{:S(2)}, u32[]{:S(2)}) collective-permute-start(bf16[2,256,256]{1,2,0:T(8,128)(2,1)S(1)} %get-tuple-element.548), channel_id=1, source_target_pairs={{0,4},{4,8},{8,12},{12,16},{16,20},{20,24},{24,28},{28,32},{32,36}... | collective-permute-start | bytes 786440 | tf_op jit(solution)/shard_map/while/body/eval_jaxpr/ppermute | solution.py:15
  253.5 13.5 %collective-permute-start = (bf16[2,256,256]{1,2,0:T(8,128)(2,1)S(1)}, bf16[2,256,256]{1,2,0:T(8,128)(2,1)S(1)}, u32[]{:S(2)}, u32[]{:S(2)}) collective-permute-start(bf16[2,256,256]{1,2,0:T(8,128)(2,1)S(1)} %get-tuple-element.548), channel_id=1, source_target_pairs={{0,4},{4,8},{8,12},{12,16},{16,20},{20,24},{24,28},{28,32},{32,36}... | collective-permute-start | bytes 786440 | tf_op jit(solution)/shard_map/while/body/eval_jaxpr/ppermute | solution.py:15
  268.9 14.6 %collective-permute-start = (bf16[2,256,256]{1,2,0:T(8,128)(2,1)S(1)}, bf16[2,256,256]{1,2,0:T(8,128)(2,1)S(1)}, u32[]{:S(2)}, u32[]{:S(2)}) collective-permute-start(bf16[2,256,256]{1,2,0:T(8,128)(2,1)S(1)} %get-tuple-element.548), channel_id=1, source_target_pairs={{0,4},{4,8},{8,12},{12,16},{16,20},{20,24},{24,28},{28,32},{32,36}... | collective-permute-start | bytes 786440 | tf_op jit(solution)/shard_map/while/body/eval_jaxpr/ppermute | solution.py:15
  285.5 15.4 %collective-permute-start = (bf16[2,256,256]{1,2,0:T(8,128)(2,1)S(1)}, bf16[2,256,256]{1,2,0:T(8,128)(2,1)S(1)}, u32[]{:S(2)}, u32[]{:S(2)}) collective-permute-start(bf16[2,256,256]{1,2,0:T(8,128)(2,1)S(1)} %get-tuple-element.548), channel_id=1, source_target_pairs={{0,4},{4,8},{8,12},{12,16},{16,20},{20,24},{24,28},{28,32},{32,36}... | collective-permute-start | bytes 786440 | tf_op jit(solution)/shard_map/while/body/eval_jaxpr/ppermute | solution.py:15
  302.7 14.5 %collective-permute-start = (bf16[2,256,256]{1,2,0:T(8,128)(2,1)S(1)}, bf16[2,256,256]{1,2,0:T(8,128)(2,1)S(1)}, u32[]{:S(2)}, u32[]{:S(2)}) collective-permute-start(bf16[2,256,256]{1,2,0:T(8,128)(2,1)S(1)} %get-tuple-element.548), channel_id=1, source_target_pairs={{0,4},{4,8},{8,12},{12,16},{16,20},{20,24},{24,28},{28,32},{32,36}... | collective-permute-start | bytes 786440 | tf_op jit(solution)/shard_map/while/body/eval_jaxpr/ppermute | solution.py:15
  319.2 13.7 %collective-permute-start = (bf16[2,256,256]{1,2,0:T(8,128)(2,1)S(1)}, bf16[2,256,256]{1,2,0:T(8,128)(2,1)S(1)}, u32[]{:S(2)}, u32[]{:S(2)}) collective-permute-start(bf16[2,256,256]{1,2,0:T(8,128)(2,1)S(1)} %get-tuple-element.548), channel_id=1, source_target_pairs={{0,4},{4,8},{8,12},{12,16},{16,20},{20,24},{24,28},{28,32},{32,36}... | collective-permute-start | bytes 786440 | tf_op jit(solution)/shard_map/while/body/eval_jaxpr/ppermute | solution.py:15
  334.7 12.8 %collective-permute-start = (bf16[2,256,256]{1,2,0:T(8,128)(2,1)S(1)}, bf16[2,256,256]{1,2,0:T(8,128)(2,1)S(1)}, u32[]{:S(2)}, u32[]{:S(2)}) collective-permute-start(bf16[2,256,256]{1,2,0:T(8,128)(2,1)S(1)} %get-tuple-element.548), channel_id=1, source_target_pairs={{0,4},{4,8},{8,12},{12,16},{16,20},{20,24},{24,28},{28,32},{32,36}... | collective-permute-start | bytes 786440 | tf_op jit(solution)/shard_map/while/body/eval_jaxpr/ppermute | solution.py:15
  349.4 12.8 %collective-permute-start = (bf16[2,256,256]{1,2,0:T(8,128)(2,1)S(1)}, bf16[2,256,256]{1,2,0:T(8,128)(2,1)S(1)}, u32[]{:S(2)}, u32[]{:S(2)}) collective-permute-start(bf16[2,256,256]{1,2,0:T(8,128)(2,1)S(1)} %get-tuple-element.548), channel_id=1, source_target_pairs={{0,4},{4,8},{8,12},{12,16},{16,20},{20,24},{24,28},{28,32},{32,36}... | collective-permute-start | bytes 786440 | tf_op jit(solution)/shard_map/while/body/eval_jaxpr/ppermute | solution.py:15
  364.1 12.8 %collective-permute-start = (bf16[2,256,256]{1,2,0:T(8,128)(2,1)S(1)}, bf16[2,256,256]{1,2,0:T(8,128)(2,1)S(1)}, u32[]{:S(2)}, u32[]{:S(2)}) collective-permute-start(bf16[2,256,256]{1,2,0:T(8,128)(2,1)S(1)} %get-tuple-element.548), channel_id=1, source_target_pairs={{0,4},{4,8},{8,12},{12,16},{16,20},{20,24},{24,28},{28,32},{32,36}... | collective-permute-start | bytes 786440 | tf_op jit(solution)/shard_map/while/body/eval_jaxpr/ppermute | solution.py:15
  378.8 12.8 %collective-permute-start = (bf16[2,256,256]{1,2,0:T(8,128)(2,1)S(1)}, bf16[2,256,256]{1,2,0:T(8,128)(2,1)S(1)}, u32[]{:S(2)}, u32[]{:S(2)}) collective-permute-start(bf16[2,256,256]{1,2,0:T(8,128)(2,1)S(1)} %get-tuple-element.548), channel_id=1, source_target_pairs={{0,4},{4,8},{8,12},{12,16},{16,20},{20,24},{24,28},{28,32},{32,36}... | collective-permute-start | bytes 786440 | tf_op jit(solution)/shard_map/while/body/eval_jaxpr/ppermute | solution.py:15
  393.5 12.8 %collective-permute-start = (bf16[2,256,256]{1,2,0:T(8,128)(2,1)S(1)}, bf16[2,256,256]{1,2,0:T(8,128)(2,1)S(1)}, u32[]{:S(2)}, u32[]{:S(2)}) collective-permute-start(bf16[2,256,256]{1,2,0:T(8,128)(2,1)S(1)} %get-tuple-element.548), channel_id=1, source_target_pairs={{0,4},{4,8},{8,12},{12,16},{16,20},{20,24},{24,28},{28,32},{32,36}... | collective-permute-start | bytes 786440 | tf_op jit(solution)/shard_map/while/body/eval_jaxpr/ppermute | solution.py:15
  408.1 12.8 %collective-permute-start = (bf16[2,256,256]{1,2,0:T(8,128)(2,1)S(1)}, bf16[2,256,256]{1,2,0:T(8,128)(2,1)S(1)}, u32[]{:S(2)}, u32[]{:S(2)}) collective-permute-start(bf16[2,256,256]{1,2,0:T(8,128)(2,1)S(1)} %get-tuple-element.548), channel_id=1, source_target_pairs={{0,4},{4,8},{8,12},{12,16},{16,20},{20,24},{24,28},{28,32},{32,36}... | collective-permute-start | bytes 786440 | tf_op jit(solution)/shard_map/while/body/eval_jaxpr/ppermute | solution.py:15
  422.8 12.8 %collective-permute-start = (bf16[2,256,256]{1,2,0:T(8,128)(2,1)S(1)}, bf16[2,256,256]{1,2,0:T(8,128)(2,1)S(1)}, u32[]{:S(2)}, u32[]{:S(2)}) collective-permute-start(bf16[2,256,256]{1,2,0:T(8,128)(2,1)S(1)} %get-tuple-element.548), channel_id=1, source_target_pairs={{0,4},{4,8},{8,12},{12,16},{16,20},{20,24},{24,28},{28,32},{32,36}... | collective-permute-start | bytes 786440 | tf_op jit(solution)/shard_map/while/body/eval_jaxpr/ppermute | solution.py:15
  437.5 12.9 %collective-permute-start = (bf16[2,256,256]{1,2,0:T(8,128)(2,1)S(1)}, bf16[2,256,256]{1,2,0:T(8,128)(2,1)S(1)}, u32[]{:S(2)}, u32[]{:S(2)}) collective-permute-start(bf16[2,256,256]{1,2,0:T(8,128)(2,1)S(1)} %get-tuple-element.548), channel_id=1, source_target_pairs={{0,4},{4,8},{8,12},{12,16},{16,20},{20,24},{24,28},{28,32},{32,36}... | collective-permute-start | bytes 786440 | tf_op jit(solution)/shard_map/while/body/eval_jaxpr/ppermute | solution.py:15
  452.3 14.0 %collective-permute-start = (bf16[2,256,256]{1,2,0:T(8,128)(2,1)S(1)}, bf16[2,256,256]{1,2,0:T(8,128)(2,1)S(1)}, u32[]{:S(2)}, u32[]{:S(2)}) collective-permute-start(bf16[2,256,256]{1,2,0:T(8,128)(2,1)S(1)} %get-tuple-element.548), channel_id=1, source_target_pairs={{0,4},{4,8},{8,12},{12,16},{16,20},{20,24},{24,28},{28,32},{32,36}... | collective-permute-start | bytes 786440 | tf_op jit(solution)/shard_map/while/body/eval_jaxpr/ppermute | solution.py:15
  468.1 15.2 %collective-permute-start = (bf16[2,256,256]{1,2,0:T(8,128)(2,1)S(1)}, bf16[2,256,256]{1,2,0:T(8,128)(2,1)S(1)}, u32[]{:S(2)}, u32[]{:S(2)}) collective-permute-start(bf16[2,256,256]{1,2,0:T(8,128)(2,1)S(1)} %get-tuple-element.548), channel_id=1, source_target_pairs={{0,4},{4,8},{8,12},{12,16},{16,20},{20,24},{24,28},{28,32},{32,36}... | collective-permute-start | bytes 786440 | tf_op jit(solution)/shard_map/while/body/eval_jaxpr/ppermute | solution.py:15
  485.2 14.8 %collective-permute-start = (bf16[2,256,256]{1,2,0:T(8,128)(2,1)S(1)}, bf16[2,256,256]{1,2,0:T(8,128)(2,1)S(1)}, u32[]{:S(2)}, u32[]{:S(2)}) collective-permute-start(bf16[2,256,256]{1,2,0:T(8,128)(2,1)S(1)} %get-tuple-element.548), channel_id=1, source_target_pairs={{0,4},{4,8},{8,12},{12,16},{16,20},{20,24},{24,28},{28,32},{32,36}... | collective-permute-start | bytes 786440 | tf_op jit(solution)/shard_map/while/body/eval_jaxpr/ppermute | solution.py:15
  502.0 14.0 %collective-permute-start = (bf16[2,256,256]{1,2,0:T(8,128)(2,1)S(1)}, bf16[2,256,256]{1,2,0:T(8,128)(2,1)S(1)}, u32[]{:S(2)}, u32[]{:S(2)}) collective-permute-start(bf16[2,256,256]{1,2,0:T(8,128)(2,1)S(1)} %get-tuple-element.548), channel_id=1, source_target_pairs={{0,4},{4,8},{8,12},{12,16},{16,20},{20,24},{24,28},{28,32},{32,36}... | collective-permute-start | bytes 786440 | tf_op jit(solution)/shard_map/while/body/eval_jaxpr/ppermute | solution.py:15
  517.9 13.1 %collective-permute-start = (bf16[2,256,256]{1,2,0:T(8,128)(2,1)S(1)}, bf16[2,256,256]{1,2,0:T(8,128)(2,1)S(1)}, u32[]{:S(2)}, u32[]{:S(2)}) collective-permute-start(bf16[2,256,256]{1,2,0:T(8,128)(2,1)S(1)} %get-tuple-element.548), channel_id=1, source_target_pairs={{0,4},{4,8},{8,12},{12,16},{16,20},{20,24},{24,28},{28,32},{32,36}... | collective-permute-start | bytes 786440 | tf_op jit(solution)/shard_map/while/body/eval_jaxpr/ppermute | solution.py:15
  532.9 12.8 %collective-permute-start = (bf16[2,256,256]{1,2,0:T(8,128)(2,1)S(1)}, bf16[2,256,256]{1,2,0:T(8,128)(2,1)S(1)}, u32[]{:S(2)}, u32[]{:S(2)}) collective-permute-start(bf16[2,256,256]{1,2,0:T(8,128)(2,1)S(1)} %get-tuple-element.548), channel_id=1, source_target_pairs={{0,4},{4,8},{8,12},{12,16},{16,20},{20,24},{24,28},{28,32},{32,36}... | collective-permute-start | bytes 786440 | tf_op jit(solution)/shard_map/while/body/eval_jaxpr/ppermute | solution.py:15
  547.6 12.8 %collective-permute-start = (bf16[2,256,256]{1,2,0:T(8,128)(2,1)S(1)}, bf16[2,256,256]{1,2,0:T(8,128)(2,1)S(1)}, u32[]{:S(2)}, u32[]{:S(2)}) collective-permute-start(bf16[2,256,256]{1,2,0:T(8,128)(2,1)S(1)} %get-tuple-element.548), channel_id=1, source_target_pairs={{0,4},{4,8},{8,12},{12,16},{16,20},{20,24},{24,28},{28,32},{32,36}... | collective-permute-start | bytes 786440 | tf_op jit(solution)/shard_map/while/body/eval_jaxpr/ppermute | solution.py:15
  562.3 12.8 %collective-permute-start = (bf16[2,256,256]{1,2,0:T(8,128)(2,1)S(1)}, bf16[2,256,256]{1,2,0:T(8,128)(2,1)S(1)}, u32[]{:S(2)}, u32[]{:S(2)}) collective-permute-start(bf16[2,256,256]{1,2,0:T(8,128)(2,1)S(1)} %get-tuple-element.548), channel_id=1, source_target_pairs={{0,4},{4,8},{8,12},{12,16},{16,20},{20,24},{24,28},{28,32},{32,36}... | collective-permute-start | bytes 786440 | tf_op jit(solution)/shard_map/while/body/eval_jaxpr/ppermute | solution.py:15
  576.9 12.8 %collective-permute-start = (bf16[2,256,256]{1,2,0:T(8,128)(2,1)S(1)}, bf16[2,256,256]{1,2,0:T(8,128)(2,1)S(1)}, u32[]{:S(2)}, u32[]{:S(2)}) collective-permute-start(bf16[2,256,256]{1,2,0:T(8,128)(2,1)S(1)} %get-tuple-element.548), channel_id=1, source_target_pairs={{0,4},{4,8},{8,12},{12,16},{16,20},{20,24},{24,28},{28,32},{32,36}... | collective-permute-start | bytes 786440 | tf_op jit(solution)/shard_map/while/body/eval_jaxpr/ppermute | solution.py:15
  591.6 12.8 %collective-permute-start = (bf16[2,256,256]{1,2,0:T(8,128)(2,1)S(1)}, bf16[2,256,256]{1,2,0:T(8,128)(2,1)S(1)}, u32[]{:S(2)}, u32[]{:S(2)}) collective-permute-start(bf16[2,256,256]{1,2,0:T(8,128)(2,1)S(1)} %get-tuple-element.548), channel_id=1, source_target_pairs={{0,4},{4,8},{8,12},{12,16},{16,20},{20,24},{24,28},{28,32},{32,36}... | collective-permute-start | bytes 786440 | tf_op jit(solution)/shard_map/while/body/eval_jaxpr/ppermute | solution.py:15
  606.3 12.8 %collective-permute-start = (bf16[2,256,256]{1,2,0:T(8,128)(2,1)S(1)}, bf16[2,256,256]{1,2,0:T(8,128)(2,1)S(1)}, u32[]{:S(2)}, u32[]{:S(2)}) collective-permute-start(bf16[2,256,256]{1,2,0:T(8,128)(2,1)S(1)} %get-tuple-element.548), channel_id=1, source_target_pairs={{0,4},{4,8},{8,12},{12,16},{16,20},{20,24},{24,28},{28,32},{32,36}... | collective-permute-start | bytes 786440 | tf_op jit(solution)/shard_map/while/body/eval_jaxpr/ppermute | solution.py:15
  641.3 31.7 %copy-start.13 = (bf16[2,1024,32]{1,2,0:T(8,128)(2,1)S(1)}, bf16[2,1024,32]{1,2,0:T(8,128)(2,1)}, u32[]{:S(2)}) copy-start(bf16[2,1024,32]{1,2,0:T(8,128)(2,1)} %param.22) | copy-start | bytes 393220
  641.3 3.0 copy-start.3
  641.3 3.1 copy-start.6
  645.7 3.2 copy-start.2
  654.6 1.8 copy-start.4
  656.4 3.0 copy-start.3
  656.4 3.0 copy-start.6
  660.8 3.2 copy-start.2
  669.8 1.8 copy-start.4
  671.5 12.1 %copy-start.14 = (f32[8]{0:T(128)S(1)}, f32[8]{0:T(128)}, u32[]{:S(2)}) copy-start(f32[8]{0:T(128)} %param.23) | copy-start | bytes 100
  672.9 11.8 %copy-start.7 = (f32[2,128,1024]{2,1,0:T(8,128)S(1)}, f32[2,128,1024]{2,1,0:T(8,128)}, u32[]{:S(2)}) copy-start(f32[2,128,1024]{2,1,0:T(8,128)} %get-tuple-element.284) | copy-start | bytes 3145732
  672.9 11.8 %copy-start.8 = (f32[256,1024]{1,0:T(8,128)S(1)}, f32[256,1024]{1,0:T(8,128)}, u32[]{:S(2)}) copy-start(f32[256,1024]{1,0:T(8,128)} %copy.86) | copy-start | bytes 3145732
  (4 other events, 6.2 us)
where the time goes:
time: 688 us; the launch traced here: 686 us
  waiting for transfers between devices  438 us (64%)
  starting transfers between devices  75.2 us (11%)
  matrix products  60.2 us (9%)
  local copies, waits for them, and re-layouts  45.3 us (7%)
  other arithmetic  34.4 us (5%)
  blocking collectives  29.5 us (4%)
    ppermute x31, waiting for transfers between devices, passed_along(): return lax.ppermute(x, axis, pairs)  389 us
    ppermute x31, starting transfers between devices, passed_along(): return lax.ppermute(x, axis, pairs)  62.5 us
    all_to_all x1, waiting for transfers between devices, on_device(): lax.all_to_all(send_keys, 'ctx', split_axis=0, concat_axis=0, tiled=True)  48.6 us
    dot_general x32, matrix products, tile_update(): jnp.einsum('kgqs,skd->kgqd', weights.astype(jnp.bfloat16), v_rows, prefer...  30.2 us
    all_to_all x1, blocking collectives, on_device(): lax.all_to_all(request, 'ctx', split_axis=0, concat_axis=0, tiled=True)  19.3 us
    dot_general x32, matrix products, tile_update(): jnp.einsum('qkgd,skd->kgqs', q_rows, k_rows, preferred_element_type=jnp.f...  17.2 us
  transfers between devices with their start and end apart: 33, of which 32 were waited for; matrix products, arithmetic and copies ran while one was open for 10% of the time, Pallas kernels for 0%

commit v1 on v0

v1 whole, which is shorter than its diff:
```python
import functools
import math

import jax
import jax.numpy as jnp
from jax import lax
from jax.experimental import pallas as pl
from jax.experimental.pallas import tpu as pltpu
from jax.sharding import PartitionSpec as P

MESH = pl.DeviceIdType.MESH
SIDE = 4
DH = 128
SHARE = 4
QBLK = 128
ROWS = 256
SHARD_BLOCKS = 32
MBLK = 64
GROUPS = 4
HEADS_DEV = 8
NEG = -1e30
FACTOR = DH**-0.5 * math.log2(math.e)


def dot_nt(a, b):
    return lax.dot_general(a, b, (((1,), (1,)), ((), ())), preferred_element_type=jnp.float32)


def with_ones(v):
    return jnp.concatenate([v, jnp.ones_like(v)], axis=1)


def rows_of(column_wide):
    eye = lax.broadcasted_iota(jnp.int32, (QBLK, QBLK), 0) == lax.broadcasted_iota(
        jnp.int32, (QBLK, QBLK), 1
    )
    pieces = []
    for g in range(SHARE):
        part = column_wide[g * QBLK : (g + 1) * QBLK]
        pieces.append(jnp.sum(jnp.where(eye, part, 0.0), axis=0, keepdims=True))
    pieces.append(jnp.zeros((8 - SHARE, QBLK), jnp.float32))
    return jnp.concatenate(pieces, axis=0)


def kernel(
    q_hbm, k_hbm, v_hbm, mk_hbm, mv_hbm, tab_hbm, gw_ref, gb_ref,
    out_ref,
    q_buf, kv_buf, mem_buf, tab_buf, tab_sm,
    loc_part, loc_lse, loc_in, loc_lse_in,
    mem_part, mem_lse, mem_in, mem_lse_in,
    z_part, z_lse, z_in, z_lse_in,
    loc_fin, mem_fin, acc_ref, max_ref, lg_out, lg_in,
    l_sem, kvz_s, kvz_r, kva_s, kva_r, qb_s, qb_r, qz_s, qz_r, tab_s, tab_r, ma_s, ma_r,
    lo_s, lo_r, ls_s, ls_r, me_s, me_r, ms_s, ms_r, z_s, z_r, zs_s, zs_r, lg_s, lg_r,
):
    c = lax.axis_index("ctx")
    g_own = lax.axis_index("mem")
    x, y, z = c // 8, (c // 2) % 4, c % 2
    zo = 1 - z

    def wrap(i):
        return lax.rem(i + SIDE, SIDE)

    def device(px, py, pz):
        return (px * 8 + py * 2 + pz, g_own)

    def key_peer(h, d):
        return device(wrap(x + d), y, z) if h == 0 else device(x, wrap(y + d), z)

    def query_peer(h, d):
        return key_peer(1 - h, d)

    z_peer = device(x, y, zo)
    a_own = (x, y)
    b_own = (y, x)

    def remote(src, dst, ssem, rsem, peer):
        return pltpu.make_async_remote_copy(
            src_ref=src, dst_ref=dst, send_sem=ssem, recv_sem=rsem,
            device_id=peer, device_id_type=MESH,
        )

    kv_local, q_local, mem_local, tab_local = [], [], [], []
    count = 0

    def local(src, dst, group):
        nonlocal count
        cp = pltpu.make_async_copy(src, dst, l_sem.at[count])
        cp.start()
        group.append(cp)
        count += 1

    for h in range(2):
        cols = pl.ds(h * DH, DH)
        local(k_hbm.at[:, cols], kv_buf.at[h, a_own[h], 0, z], kv_local)
        local(v_hbm.at[:, cols], kv_buf.at[h, a_own[h], 1, z], kv_local)
    for h in range(2):
        for g in range(SHARE):
            local(
                q_hbm.at[:, pl.ds((h * SHARE + g) * DH, DH)],
                q_buf.at[h, b_own[h], z, g],
                q_local,
            )
        local(tab_hbm, tab_buf.at[h, b_own[h], z], tab_local)
    for h in range(2):
        cols = pl.ds(h * DH, DH)
        local(mk_hbm.at[:, :, cols], mem_buf.at[h, a_own[h], 0], mem_local)
        local(mv_hbm.at[:, :, cols], mem_buf.at[h, a_own[h], 1], mem_local)

    barrier = pltpu.get_barrier_semaphore()
    greeted = [z_peer]
    for d in range(1, SIDE):
        greeted += [device(wrap(x + d), y, z), device(x, wrap(y + d), z)]
        greeted += [device(wrap(x + d), y, zo), device(x, wrap(y + d), zo)]
        greeted += [(c, lax.rem(g_own + d, GROUPS))]
    for peer in greeted:
        pl.semaphore_signal(barrier, inc=1, device_id=peer, device_id_type=MESH)
    pl.semaphore_wait(barrier, len(greeted))

    started = []

    def go(cp):
        cp.start()
        started.append(cp)
        return cp

    def kv_z(h):
        ref = kv_buf.at[h, a_own[h], :, z]
        return remote(ref, ref, kvz_s.at[h], kvz_r.at[h], z_peer)

    def kv_z_in(h):
        ref = kv_buf.at[h, a_own[h], :, zo]
        return remote(ref, ref, kvz_s.at[h], kvz_r.at[h], z_peer)

    def kv_a(h, part, d):
        ref = kv_buf.at[h, a_own[h], :, (z, zo)[part]]
        return remote(ref, ref, kva_s.at[h, part, d], kva_r.at[h, part, d], key_peer(h, d))

    def kv_a_in(h, part, d):
        ref = kv_buf.at[h, wrap(a_own[h] - d), :, (z, zo)[part]]
        return remote(ref, ref, kva_s.at[h, part, d], kva_r.at[h, part, d], key_peer(h, d))

    def q_b(h, d):
        ref = q_buf.at[h, b_own[h], z]
        return remote(ref, ref, qb_s.at[h, d], qb_r.at[h, d], query_peer(h, d))

    def q_b_in(h, d):
        ref = q_buf.at[h, wrap(b_own[h] - d), z]
        return remote(ref, ref, qb_s.at[h, d], qb_r.at[h, d], query_peer(h, d))

    def q_z(h, d):
        ref = q_buf.at[h, wrap(b_own[h] + d), z]
        return remote(ref, ref, qz_s.at[h, d], qz_r.at[h, d], z_peer)

    def q_z_in(h, d):
        ref = q_buf.at[h, wrap(b_own[h] + d), zo]
        return remote(ref, ref, qz_s.at[h, d], qz_r.at[h, d], z_peer)

    def tab_peer(h, d, dz):
        pz = zo if dz else z
        return device(x, wrap(y + d), pz) if h == 0 else device(wrap(x + d), y, pz)

    def tab(h, d, dz):
        ref = tab_buf.at[h, b_own[h], z]
        sem = d * 2 + dz
        return remote(ref, ref, tab_s.at[h, sem], tab_r.at[h, sem], tab_peer(h, d, dz))

    def tab_in(h, d, dz):
        ref = tab_buf.at[h, wrap(b_own[h] - d), zo if dz else z]
        sem = d * 2 + dz
        return remote(ref, ref, tab_s.at[h, sem], tab_r.at[h, sem], tab_peer(h, d, dz))

    def mem_copy(h, which, ref, d):
        return remote(ref, ref, ma_s.at[h, which], ma_r.at[h, which], key_peer(h, d))

    for cp in kv_local:
        cp.wait()
    for h in range(2):
        go(kv_z(h))
    for d in (2, 1, 3):
        for h in range(2):
            go(kv_a(h, 0, d))
    for cp in q_local:
        cp.wait()
    for d in (2, 1, 3):
        for h in range(2):
            go(q_b(h, d))
    for h in range(2):
        go(q_z(h, 0))
    for cp in tab_local:
        cp.wait()
    for h in range(2):
        for d in range(SIDE):
            for dz in range(2):
                if d or dz:
                    go(tab(h, d, dz))
    for cp in mem_local:
        cp.wait()
    for h in range(2):
        own_k, own_v = mem_buf.at[h, a_own[h], 0], mem_buf.at[h, a_own[h], 1]
        go(mem_copy(h, 0, own_k, 1))
        go(mem_copy(h, 1, own_v, 3))
    for h in range(2):
        own_k, own_v = mem_buf.at[h, a_own[h], 0], mem_buf.at[h, a_own[h], 1]
        go(mem_copy(h, 2, own_v, 1))
        go(mem_copy(h, 3, own_k, 3))

    for h in range(2):
        kv_z_in(h).wait_recv()
    for d in (2, 1, 3):
        for h in range(2):
            go(kv_a(h, 1, d))
    for d in (1, 3, 2):
        for h in range(2):
            q_b_in(h, d).wait_recv()
            go(q_z(h, SIDE - d))
    for d in (1, 3, 2):
        for h in range(2):
            kv_a_in(h, 0, d).wait_recv()
            kv_a_in(h, 1, d).wait_recv()

    def local_shard(h, d):
        b = wrap(b_own[h] + d)
        if h == 0:
            tiles = x + jnp.where(y <= b, 1, 0)
            q_shard = (x * 4 + b) * 2 + z
        else:
            tiles = jnp.where(x < b, 4, jnp.where(x == b, y + 1, 0))
            q_shard = (b * 4 + y) * 2 + z
        lane_blk = lax.broadcasted_iota(jnp.int32, (1, 512), 1) // QBLK

        def block(blk, carry):
            tok = pl.ds(pl.multiple_of(blk * QBLK, QBLK), QBLK)
            q4 = q_buf[h, b, z, :, tok, :].reshape(SHARE * QBLK, DH)
            acc_ref[...] = jnp.zeros_like(acc_ref)
            max_ref[...] = jnp.full_like(max_ref, NEG)

            def tile(a, inner):
                k_shard = (a * 4 + y) * 2 if h == 0 else (x * 4 + a) * 2
                keys = kv_buf[h, a, 0].reshape(512, DH)
                vals = kv_buf[h, a, 1].reshape(512, DH)
                seen = k_shard * 2 + lane_blk <= q_shard * 2 + blk
                s = dot_nt(q4, keys) + jnp.where(seen, 0.0, NEG)
                old = max_ref[...]
                new = jnp.maximum(old, jnp.max(s, axis=1, keepdims=True))
                wide = jnp.concatenate([new] * 4, axis=1)
                p = jnp.exp2((s - wide) * FACTOR).astype(jnp.bfloat16)
                fade = jnp.exp2((old - new) * FACTOR)
                add = jnp.dot(p, with_ones(vals), preferred_element_type=jnp.float32)
                acc_ref[:, :DH] = acc_ref[:, :DH] * fade + add[:, :DH]
                acc_ref[:, DH:] = acc_ref[:, DH:] * fade + add[:, DH:]
                max_ref[...] = new
                return inner

            lax.fori_loop(0, tiles, tile, 0)
            total = acc_ref[:, DH:]
            some = total > 0.0
            safe = jnp.where(some, total, 1.0)
            result = acc_ref[:, :DH] / safe
            loc_part[h, b, :, tok, :] = result.astype(jnp.bfloat16).reshape(SHARE, QBLK, DH)
            lse = jnp.where(some, max_ref[...] * FACTOR + jnp.log2(safe), NEG)
            loc_lse[h, b, :, tok] = rows_of(lse)
            return carry

        lax.fori_loop(0, 2, block, 0)

    def loc_out(h, d):
        b = wrap(b_own[h] + d)
        return (
            remote(loc_part.at[h, b], loc_in.at[h, d], lo_s.at[h, d], lo_r.at[h, d], query_peer(h, d)),
            remote(loc_lse.at[h, b], loc_lse_in.at[h, d], ls_s.at[h, d], ls_r.at[h, d], query_peer(h, d)),
        )

    for d in (2, 1, 3, 0):
        for h in range(2):
            local_shard(h, d)
            if d:
                for cp in loc_out(h, d):
                    go(cp)
        if d == 2:
            for h in range(2):
                left, right = wrap(a_own[h] - 1), wrap(a_own[h] + 1)
                mem_copy(h, 0, mem_buf.at[h, left, 0], 1).wait_recv()
                go(mem_copy(h, 4, mem_buf.at[h, left, 0], 1))
                mem_copy(h, 1, mem_buf.at[h, right, 1], 3).wait_recv()
                go(mem_copy(h, 5, mem_buf.at[h, right, 1], 3))

    for h in range(2):
        for d in range(SIDE):
            for dz in range(2):
                if d or dz:
                    tab_in(h, d, dz).wait_recv()
    to_smem = pltpu.make_async_copy(tab_buf, tab_sm, l_sem.at[count])
    to_smem.start()
    to_smem.wait()
    for h in range(2):
        left, right = wrap(a_own[h] - 1), wrap(a_own[h] + 1)
        across = wrap(a_own[h] + 2)
        mem_copy(h, 2, mem_buf.at[h, left, 1], 1).wait_recv()
        mem_copy(h, 3, mem_buf.at[h, right, 0], 3).wait_recv()
        mem_copy(h, 4, mem_buf.at[h, across, 0], 1).wait_recv()
        mem_copy(h, 5, mem_buf.at[h, across, 1], 3).wait_recv()
        for d in range(SIDE):
            q_z_in(h, d).wait_recv()

    lane = lax.broadcasted_iota(jnp.int32, (1, 2 * MBLK), 1)

    def memory_shard(h, b, pz):
        def block(blk, carry):
            tok = pl.ds(pl.multiple_of(blk * QBLK, QBLK), QBLK)
            q4 = q_buf[h, b, pz, :, tok, :].reshape(SHARE * QBLK, DH)
            keys, vals, bias = [], [], []
            for a in range(SIDE):
                shard = (a * 4 + y) * 2 + z if h == 0 else (x * 4 + a) * 2 + z
                slots = [tab_sm[h, b, pz, blk, shard * 2 + k] for k in range(2)]
                for slot in slots:
                    at = jnp.maximum(slot, 0)
                    keys.append(mem_buf[h, a, 0, at])
                    vals.append(mem_buf[h, a, 1, at])
                off = [jnp.where(slot < 0, NEG, 0.0) for slot in slots]
                bias.append(jnp.where(lane < MBLK, off[0], off[1]))
            s = dot_nt(q4, jnp.concatenate(keys, axis=0)) + jnp.concatenate(bias, axis=1)
            top = jnp.max(s, axis=1, keepdims=True)
            p = jnp.exp2((s - top) * FACTOR).astype(jnp.bfloat16)
            both = jnp.dot(
                p, with_ones(jnp.concatenate(vals, axis=0)), preferred_element_type=jnp.float32
            )
            total = both[:, DH:]
            result = both[:, :DH] / total
            mem_part[h, b, pz, :, tok, :] = result.astype(jnp.bfloat16).reshape(SHARE, QBLK, DH)
            mem_lse[h, b, pz, :, tok] = rows_of(top * FACTOR + jnp.log2(total))
            return carry

        lax.fori_loop(0, 2, block, 0)

    def mem_out(h, part, d):
        b, pz = wrap(b_own[h] + d), (zo, z)[part]
        return (
            remote(mem_part.at[h, b, pz], mem_in.at[h, part, d], me_s.at[h, part, d], me_r.at[h, part, d], query_peer(h, d)),
            remote(mem_lse.at[h, b, pz], mem_lse_in.at[h, part, d], ms_s.at[h, part, d], ms_r.at[h, part, d], query_peer(h, d)),
        )

    def weights(stats):
        top = functools.reduce(jnp.maximum, stats)
        powers = [jnp.exp2(s - top) for s in stats]
        total = functools.reduce(jnp.add, powers)
        scales = [jnp.transpose(p / total) for p in powers]
        return scales, top + jnp.log2(total)

    def merge(parts, scales, g):
        total = None
        for part, scale in zip(parts, scales):
            term = part(g).astype(jnp.float32) * scale[:, g : g + 1]
            total = term if total is None else total + term
        return total

    for part in range(2):
        pz = (zo, z)[part]
        for d in (2, 1, 3, 0):
            for h in range(2):
                memory_shard(h, wrap(b_own[h] + d), pz)
                if d:
                    for cp in mem_out(h, part, d):
                        go(cp)

    for h in range(2):
        for d in range(1, SIDE):
            for cp in loc_out(h, d):
                cp.wait_recv()
        stats = [loc_lse[h, b_own[h]]] + [loc_lse_in[h, d] for d in range(1, SIDE)]
        scales, _ = weights(stats)
        parts = [lambda g, h=h: loc_part[h, b_own[h], g]]
        parts += [lambda g, h=h, d=d: loc_in[h, d, g] for d in range(1, SIDE)]
        for g in range(SHARE):
            loc_fin[h * SHARE + g] = merge(parts, scales, g)

    for part in range(2):
        pz = (zo, z)[part]
        for h in range(2):
            for d in range(1, SIDE):
                for cp in mem_out(h, part, d):
                    cp.wait_recv()
            stats = [mem_lse[h, b_own[h], pz]]
            stats += [mem_lse_in[h, part, d] for d in range(1, SIDE)]
            parts = [lambda g, h=h, pz=pz: mem_part[h, b_own[h], pz, g]]
            parts += [lambda g, h=h, d=d, part=part: mem_in[h, part, d, g] for d in range(1, SIDE)]
            z_data = remote(z_part.at[h], z_in.at[h], z_s.at[h], z_r.at[h], z_peer)
            z_stat = remote(z_lse.at[h], z_lse_in.at[h], zs_s.at[h], zs_r.at[h], z_peer)
            if part == 1:
                z_data.wait_recv()
                z_stat.wait_recv()
                stats.append(z_lse_in[h])
                parts.append(lambda g, h=h: z_in[h, g])
            scales, whole = weights(stats)
            for g in range(SHARE):
                result = merge(parts, scales, g)
                if part == 0:
                    z_part[h, g] = result.astype(jnp.bfloat16)
                else:
                    mem_fin[h * SHARE + g] = result
            if part == 0:
                z_lse[h] = whole
                go(z_data)
                go(z_stat)

    logits = jnp.zeros((ROWS, GROUPS * HEADS_DEV), jnp.float32)
    for head in range(HEADS_DEV):
        feats = pl.ds(head * DH, DH)
        logits += jnp.dot(
            loc_fin[head].astype(jnp.bfloat16), gw_ref[0, feats, :], preferred_element_type=jnp.float32
        )
        logits += jnp.dot(
            mem_fin[head].astype(jnp.bfloat16), gw_ref[1, feats, :], preferred_element_type=jnp.float32
        )
    lg_out[...] = jnp.transpose(logits).reshape(GROUPS, HEADS_DEV, ROWS)

    def lg(d):
        to = lax.rem(g_own + d, GROUPS)
        return remote(lg_out.at[to], lg_in.at[d], lg_s.at[d], lg_r.at[d], (c, to))

    for d in range(1, GROUPS):
        go(lg(d))
    own = lg_out[g_own]
    for d in range(1, GROUPS):
        lg(d).wait_recv()
        own = own + lg_in[d]
    gate = jax.nn.sigmoid(jnp.transpose(own) + gb_ref[...])
    for head in range(HEADS_DEV):
        share = gate[:, head : head + 1]
        mixed = share * mem_fin[head] + (1.0 - share) * loc_fin[head]
        out_ref[:, head * DH : (head + 1) * DH] = mixed.astype(jnp.bfloat16)

    for cp in started:
        cp.wait_send()


def block_table(retrieval):
    ids = retrieval.reshape(2, -1)
    owner, offset = ids // SHARD_BLOCKS, ids % SHARD_BLOCKS
    here = owner[:, None, :] == jnp.arange(32, dtype=jnp.int32)[None, :, None]
    held = jnp.sum(here.astype(jnp.int32), axis=2)
    low = jnp.min(jnp.where(here, offset[:, None, :], SHARD_BLOCKS), axis=2)
    high = jnp.max(jnp.where(here, offset[:, None, :], -1), axis=2)
    first = jnp.where(held > 0, low, -1)
    second = jnp.where(held > 1, high, -1)
    both = jnp.stack([first, second], axis=2).reshape(2, 64)
    return jnp.pad(both, ((0, 6), (0, 64)))


def on_device(queries, keys, values, mem_keys, mem_values, retrieval, gate_weight, gate_bias):
    bf, f32 = jnp.bfloat16, jnp.float32
    dma = pltpu.SemaphoreType.DMA
    anywhere = pl.BlockSpec(memory_space=pl.ANY)
    vmem = pl.BlockSpec(memory_space=pltpu.VMEM)
    part = (SHARE, ROWS, DH)
    stat = (8, ROWS)
    return pl.pallas_call(
        kernel,
        out_shape=jax.ShapeDtypeStruct((ROWS, HEADS_DEV * DH), bf),
        in_specs=[anywhere] * 6 + [vmem] * 2,
        out_specs=vmem,
        scratch_shapes=[
            pltpu.VMEM((2, SIDE, 2) + part, bf),
            pltpu.VMEM((2, SIDE, 2, 2, ROWS, DH), bf),
            pltpu.VMEM((2, SIDE, 2, SHARD_BLOCKS, MBLK, DH), bf),
            pltpu.VMEM((2, SIDE, 2, 8, 128), jnp.int32),
            pltpu.SMEM((2, SIDE, 2, 8, 128), jnp.int32),
            pltpu.VMEM((2, SIDE) + part, bf),
            pltpu.VMEM((2, SIDE) + stat, f32),
            pltpu.VMEM((2, SIDE) + part, bf),
            pltpu.VMEM((2, SIDE) + stat, f32),
            pltpu.VMEM((2, SIDE, 2) + part, bf),
            pltpu.VMEM((2, SIDE, 2) + stat, f32),
            pltpu.VMEM((2, 2, SIDE) + part, bf),
            pltpu.VMEM((2, 2, SIDE) + stat, f32),
            pltpu.VMEM((2,) + part, bf),
            pltpu.VMEM((2,) + stat, f32),
            pltpu.VMEM((2,) + part, bf),
            pltpu.VMEM((2,) + stat, f32),
            pltpu.VMEM((HEADS_DEV, ROWS, DH), f32),
            pltpu.VMEM((HEADS_DEV, ROWS, DH), f32),
            pltpu.VMEM((SHARE * QBLK, 2 * DH), f32),
            pltpu.VMEM((SHARE * QBLK, DH), f32),
            pltpu.VMEM((GROUPS, HEADS_DEV, ROWS), f32),
            pltpu.VMEM((GROUPS, HEADS_DEV, ROWS), f32),
            dma((24,)),
            dma((2,)), dma((2,)),
            dma((2, 2, SIDE)), dma((2, 2, SIDE)),
            dma((2, SIDE)), dma((2, SIDE)),
            dma((2, SIDE)), dma((2, SIDE)),
            dma((2, 8)), dma((2, 8)),
            dma((2, 6)), dma((2, 6)),
            dma((2, SIDE)), dma((2, SIDE)),
            dma((2, SIDE)), dma((2, SIDE)),
            dma((2, 2, SIDE)), dma((2, 2, SIDE)),
            dma((2, 2, SIDE)), dma((2, 2, SIDE)),
            dma((2,)), dma((2,)),
            dma((2,)), dma((2,)),
            dma((SIDE,)), dma((SIDE,)),
        ],
        compiler_params=pltpu.CompilerParams(
            collective_id=0, has_side_effects=True, vmem_limit_bytes=60 * 2**20
        ),
    )(
        queries, keys, values, mem_keys, mem_values, block_table(retrieval),
        gate_weight, gate_bias.reshape(1, HEADS_DEV),
    )


def solution(mesh):
    placed = (
        P("ctx", "mem"),
        P("ctx", "mem"),
        P("ctx", "mem"),
        P("ctx", None, "mem"),
        P("ctx", None, "mem"),
        P("ctx", "mem", None),
        P(None, "mem", None),
        P("mem"),
    )
    return jax.shard_map(
        on_device, mesh=mesh, in_specs=placed, out_specs=P("ctx", "mem"), check_vma=False
    )
```

time: 688 us -> 143 us (0.21)
  the two profiles are of different devices: /device:TPU:2 before, /device:TPU:1 now
where the time goes in v1:
time: 143 us; the launch traced here: 142 us
  Pallas kernels  137 us (96%)
  local copies, waits for them, and re-layouts  5.26 us (4%)
    pallas_call x1, Pallas kernels, on_device(): pl.pallas_call(kernel, out_shape=jax.ShapeDtypeStruct((ROWS, HEADS_DEV *...  137 us
    unnamed x4, local copies, waits for them, and re-layouts  4.45 us

profile of v1, /device:TPU:1, one launch (start us, length us, event | category | flops | bytes accessed | tf_op | source)
XLA Modules:
  0.0 142.4 jit_solution(9051796367960905501)
XLA Ops:
  0.0 0.0 copy-start
  0.0 0.7 copy-done
  0.7 0.2 select_reduce_fusion.1
  0.9 0.1 copy.13
  1.0 0.1 reshape.43
  1.1 0.6 pad.4.tab_hbm
  1.7 1.9 %copy.14.gw_ref = bf16[2,1024,32]{2,1,0:T(8,128)(2,1)} copy(bf16[2,1024,32]{1,2,0:T(8,128)(2,1)} %param.14) | data formatting | bytes 262144 | tf_op args[6]
  3.6 136.9 %shard_map.82 = bf16[256,1024]{1,0:T(8,128)(2,1)} custom-call(bf16[256,1024]{1,0:T(8,128)(2,1)} %q_hbm.1, bf16[256,256]{1,0:T(8,128)(2,1)} %k_hbm.1, bf16[256,256]{1,0:T(8,128)(2,1)} %v_hbm.1, bf16[32,64,256]{2,1,0:T(8,128)(2,1)} %mk_hbm.1, bf16[32,64,256]{2,1,0:T(8,128)(2,1)} %mv_hbm.1, s32[8,128]{1,0:T(8,128)} %pad.4.tab_hbm, ...), custom_call_target="tpu_custom_call" | custom-call | tf_op jit(solution)/shard_map/pallas_call | solution.py:457
  140.5 1.9 %copy.16 = bf16[256,1024]{1,0:T(8,128)(2,1)} copy(bf16[256,1024]{1,0:T(8,128)(2,1)} %shard_map.82) | data formatting | bytes 1048576
  (4 shorter events, 0.0 us)
Async XLA Ops:
  0.0 0.7 copy-start

commit v2 on v1

--- a/solution.py
+++ b/solution.py
@@ -30,20 +30,33 @@
     return jnp.concatenate([v, jnp.ones_like(v)], axis=1)
 
 
-def rows_of(column_wide):
-    eye = lax.broadcasted_iota(jnp.int32, (QBLK, QBLK), 0) == lax.broadcasted_iota(
-        jnp.int32, (QBLK, QBLK), 1
-    )
-    pieces = []
-    for g in range(SHARE):
-        part = column_wide[g * QBLK : (g + 1) * QBLK]
-        pieces.append(jnp.sum(jnp.where(eye, part, 0.0), axis=0, keepdims=True))
-    pieces.append(jnp.zeros((8 - SHARE, QBLK), jnp.float32))
-    return jnp.concatenate(pieces, axis=0)
+def rows_of(pieces):
+    shape = (QBLK, QBLK)
+    eye = lax.broadcasted_iota(jnp.int32, shape, 0) == lax.broadcasted_iota(jnp.int32, shape, 1)
+    rows = [jnp.sum(jnp.where(eye, piece, 0.0), axis=0, keepdims=True) for piece in pieces]
+    return jnp.concatenate(rows + [jnp.zeros((8 - SHARE, QBLK), jnp.float32)], axis=0)
+
+
+def block_table(ids):
+    shape = (SHARD_BLOCKS, SHARD_BLOCKS)
+    shard = lax.broadcasted_iota(jnp.int32, shape, 0)
+    lane = lax.broadcasted_iota(jnp.int32, (SHARD_BLOCKS, 128), 1)
+    table = jnp.full((SHARD_BLOCKS, 128), -1, jnp.int32)
+    for l in range(2):
+        row = ids[l : l + 1, :]
+        held = row // SHARD_BLOCKS == shard
+        offset = row % SHARD_BLOCKS + jnp.zeros_like(shard)
+        low = jnp.min(jnp.where(held, offset, 99), axis=1, keepdims=True)
+        high = jnp.max(jnp.where(held, offset, -1), axis=1, keepdims=True)
+        first = jnp.where(low > 90, -1, low)
+        second = jnp.where(high > low, high, -1)
+        table = jnp.where(lane == 2 * l, first, jnp.where(lane == 2 * l + 1, second, table))
+    turned = jnp.transpose(table)[:8]
+    return jnp.concatenate([turned, jnp.full((8, 96), -1, jnp.int32)], axis=1)
 
 
 def kernel(
-    q_hbm, k_hbm, v_hbm, mk_hbm, mv_hbm, tab_hbm, gw_ref, gb_ref,
+    q_hbm, k_hbm, v_hbm, mk_hbm, mv_hbm, ids_ref, gw_ref, gb_ref,
     out_ref,
     q_buf, kv_buf, mem_buf, tab_buf, tab_sm,
     loc_part, loc_lse, loc_in, loc_lse_in,
@@ -80,7 +93,7 @@
             device_id=peer, device_id_type=MESH,
         )
 
-    kv_local, q_local, mem_local, tab_local = [], [], [], []
+    kv_local, q_local, mem_local = [], [], []
     count = 0
 
     def local(src, dst, group):
@@ -101,7 +114,6 @@
                 q_buf.at[h, b_own[h], z, g],
                 q_local,
             )
-        local(tab_hbm, tab_buf.at[h, b_own[h], z], tab_local)
     for h in range(2):
         cols = pl.ds(h * DH, DH)
         local(mk_hbm.at[:, :, cols], mem_buf.at[h, a_own[h], 0], mem_local)
@@ -132,21 +144,38 @@
         ref = kv_buf.at[h, a_own[h], :, zo]
         return remote(ref, ref, kvz_s.at[h], kvz_r.at[h], z_peer)
 
-    def kv_a(h, part, d):
-        ref = kv_buf.at[h, a_own[h], :, (z, zo)[part]]
-        return remote(ref, ref, kva_s.at[h, part, d], kva_r.at[h, part, d], key_peer(h, d))
-
-    def kv_a_in(h, part, d):
-        ref = kv_buf.at[h, wrap(a_own[h] - d), :, (z, zo)[part]]
-        return remote(ref, ref, kva_s.at[h, part, d], kva_r.at[h, part, d], key_peer(h, d))
-
-    def q_b(h, d):
-        ref = q_buf.at[h, b_own[h], z]
-        return remote(ref, ref, qb_s.at[h, d], qb_r.at[h, d], query_peer(h, d))
-
-    def q_b_in(h, d):
-        ref = q_buf.at[h, wrap(b_own[h] - d), z]
-        return remote(ref, ref, qb_s.at[h, d], qb_r.at[h, d], query_peer(h, d))
+    def ring(h, own, peer, ref, ssem, rsem):
+        left, right, across = wrap(own - 1), wrap(own + 1), wrap(own + 2)
+        out = [(own, 0, 1), (own, 1, 3), (own, 1, 1), (own, 0, 3), (left, 0, 1), (right, 1, 3)]
+        come = [(left, 0), (right, 1), (left, 1), (right, 0), (across, 0), (across, 1)]
+
+        def send(n):
+            at, half, d = out[n]
+            go(remote(ref(at, half), ref(at, half), ssem.at[n], rsem.at[n], peer(h, d)))
+
+        def wait(n):
+            at, half = come[n]
+            remote(ref(at, half), ref(at, half), ssem.at[n], rsem.at[n], z_peer).wait_recv()
+
+        return send, wait
+
+    def kv_ring(h, part):
+        pz = (z, zo)[part]
+        return ring(
+            h, a_own[h], key_peer, lambda at, half: kv_buf.at[h, at, half, pz],
+            kva_s.at[h, part], kva_r.at[h, part],
+        )
+
+    def q_ring(h):
+        return ring(
+            h, b_own[h], query_peer, lambda at, half: q_buf.at[h, at, z, pl.ds(2 * half, 2)],
+            qb_s.at[h], qb_r.at[h],
+        )
+
+    def mem_ring(h):
+        return ring(
+            h, a_own[h], key_peer, lambda at, half: mem_buf.at[h, at, half], ma_s.at[h], ma_r.at[h]
+        )
 
     def q_z(h, d):
         ref = q_buf.at[h, wrap(b_own[h] + d), z]
@@ -170,54 +199,59 @@
         sem = d * 2 + dz
         return remote(ref, ref, tab_s.at[h, sem], tab_r.at[h, sem], tab_peer(h, d, dz))
 
-    def mem_copy(h, which, ref, d):
-        return remote(ref, ref, ma_s.at[h, which], ma_r.at[h, which], key_peer(h, d))
-
+    q_rings = [q_ring(h) for h in range(2)]
+    kv_rings = [kv_ring(h, 0) for h in range(2)]
+    kvo_rings = [kv_ring(h, 1) for h in range(2)]
+    mem_rings = [mem_ring(h) for h in range(2)]
+
+    def on(rings, what, *steps):
+        for n in steps:
+            for r in rings:
+                r[what](n)
+
+    SEND, WAIT = 0, 1
     for cp in kv_local:
         cp.wait()
     for h in range(2):
         go(kv_z(h))
-    for d in (2, 1, 3):
-        for h in range(2):
-            go(kv_a(h, 0, d))
     for cp in q_local:
         cp.wait()
-    for d in (2, 1, 3):
-        for h in range(2):
-            go(q_b(h, d))
+    on(q_rings, SEND, 0, 1)
+    on(kv_rings, SEND, 0, 1)
+    on(q_rings, SEND, 2, 3)
+    on(kv_rings, SEND, 2, 3)
     for h in range(2):
         go(q_z(h, 0))
-    for cp in tab_local:
+    for cp in mem_local:
         cp.wait()
+    on(mem_rings, SEND, 0, 1)
+    for h in range(2):
+        tab_buf[h, b_own[h], z] = block_table(ids_ref[...])
     for h in range(2):
         for d in range(SIDE):
             for dz in range(2):
                 if d or dz:
                     go(tab(h, d, dz))
-    for cp in mem_local:
-        cp.wait()
-    for h in range(2):
-        own_k, own_v = mem_buf.at[h, a_own[h], 0], mem_buf.at[h, a_own[h], 1]
-        go(mem_copy(h, 0, own_k, 1))
-        go(mem_copy(h, 1, own_v, 3))
-    for h in range(2):
-        own_k, own_v = mem_buf.at[h, a_own[h], 0], mem_buf.at[h, a_own[h], 1]
-        go(mem_copy(h, 2, own_v, 1))
-        go(mem_copy(h, 3, own_k, 3))
-
+
+    on(q_rings, WAIT, 0, 1)
+    on(q_rings, SEND, 4, 5)
+    on(kv_rings, WAIT, 0, 1)
+    on(kv_rings, SEND, 4, 5)
     for h in range(2):
         kv_z_in(h).wait_recv()
-    for d in (2, 1, 3):
-        for h in range(2):
-            go(kv_a(h, 1, d))
-    for d in (1, 3, 2):
-        for h in range(2):
-            q_b_in(h, d).wait_recv()
-            go(q_z(h, SIDE - d))
-    for d in (1, 3, 2):
-        for h in range(2):
-            kv_a_in(h, 0, d).wait_recv()
-            kv_a_in(h, 1, d).wait_recv()
+    on(kvo_rings, SEND, 0, 1, 2, 3)
+    on(mem_rings, SEND, 2, 3)
+    on(q_rings, WAIT, 2, 3)
+    for h in range(2):
+        go(q_z(h, 1))
+        go(q_z(h, 3))
+    on(kvo_rings, WAIT, 0, 1)
+    on(kvo_rings, SEND, 4, 5)
+    on(q_rings, WAIT, 4, 5)
+    for h in range(2):
+        go(q_z(h, 2))
+    on(kv_rings, WAIT, 2, 3, 4, 5)
+    on(kvo_rings, WAIT, 2, 3, 4, 5)
 
     def local_shard(h, d):
         b = wrap(b_own[h] + d)
@@ -229,40 +263,43 @@
             q_shard = (b * 4 + y) * 2 + z
         lane_blk = lax.broadcasted_iota(jnp.int32, (1, 512), 1) // QBLK
 
-        def block(blk, carry):
-            tok = pl.ds(pl.multiple_of(blk * QBLK, QBLK), QBLK)
-            q4 = q_buf[h, b, z, :, tok, :].reshape(SHARE * QBLK, DH)
-            acc_ref[...] = jnp.zeros_like(acc_ref)
-            max_ref[...] = jnp.full_like(max_ref, NEG)
-
-            def tile(a, inner):
-                k_shard = (a * 4 + y) * 2 if h == 0 else (x * 4 + a) * 2
-                keys = kv_buf[h, a, 0].reshape(512, DH)
-                vals = kv_buf[h, a, 1].reshape(512, DH)
+        acc_ref[...] = jnp.zeros_like(acc_ref)
+        max_ref[...] = jnp.full_like(max_ref, NEG)
+
+        def tile(a, carry):
+            k_shard = (a * 4 + y) * 2 if h == 0 else (x * 4 + a) * 2
+            keys = kv_buf[h, a, 0].reshape(512, DH)
+            vals = with_ones(kv_buf[h, a, 1].reshape(512, DH))
+            for blk in range(2):
                 seen = k_shard * 2 + lane_blk <= q_shard * 2 + blk
-                s = dot_nt(q4, keys) + jnp.where(seen, 0.0, NEG)
-                old = max_ref[...]
-                new = jnp.maximum(old, jnp.max(s, axis=1, keepdims=True))
-                wide = jnp.concatenate([new] * 4, axis=1)
-                p = jnp.exp2((s - wide) * FACTOR).astype(jnp.bfloat16)
-                fade = jnp.exp2((old - new) * FACTOR)
-                add = jnp.dot(p, with_ones(vals), preferred_element_type=jnp.float32)
-                acc_ref[:, :DH] = acc_ref[:, :DH] * fade + add[:, :DH]
-                acc_ref[:, DH:] = acc_ref[:, DH:] * fade + add[:, DH:]
-                max_ref[...] = new
-                return inner
-
-            lax.fori_loop(0, tiles, tile, 0)
-            total = acc_ref[:, DH:]
-            some = total > 0.0
-            safe = jnp.where(some, total, 1.0)
-            result = acc_ref[:, :DH] / safe
-            loc_part[h, b, :, tok, :] = result.astype(jnp.bfloat16).reshape(SHARE, QBLK, DH)
-            lse = jnp.where(some, max_ref[...] * FACTOR + jnp.log2(safe), NEG)
-            loc_lse[h, b, :, tok] = rows_of(lse)
+                bias = jnp.where(seen, 0.0, NEG)
+                for g in range(SHARE):
+                    n = blk * SHARE + g
+                    q = q_buf[h, b, z, g, blk * QBLK : (blk + 1) * QBLK, :]
+                    s = dot_nt(q, keys) + bias
+                    old = max_ref[n]
+                    new = jnp.maximum(old, jnp.max(s, axis=1, keepdims=True))
+                    wide = jnp.concatenate([new] * 4, axis=1)
+                    p = jnp.exp2((s - wide) * FACTOR).astype(jnp.bfloat16)
+                    fade = jnp.exp2((old - new) * FACTOR)
+                    add = jnp.dot(p, vals, preferred_element_type=jnp.float32)
+                    acc_ref[n, :, :DH] = acc_ref[n, :, :DH] * fade + add[:, :DH]
+                    acc_ref[n, :, DH:] = acc_ref[n, :, DH:] * fade + add[:, DH:]
+                    max_ref[n] = new
             return carry
 
-        lax.fori_loop(0, 2, block, 0)
+        lax.fori_loop(0, tiles, tile, 0)
+        for blk in range(2):
+            tok = slice(blk * QBLK, (blk + 1) * QBLK)
+            sums = []
+            for g in range(SHARE):
+                n = blk * SHARE + g
+                total = acc_ref[n, :, DH:]
+                some = total > 0.0
+                safe = jnp.where(some, total, 1.0)
+                loc_part[h, b, g, tok, :] = (acc_ref[n, :, :DH] / safe).astype(jnp.bfloat16)
+                sums.append(jnp.where(some, max_ref[n] * FACTOR + jnp.log2(safe), NEG))
+            loc_lse[h, b, :, tok] = rows_of(sums)
 
     def loc_out(h, d):
         b = wrap(b_own[h] + d)
@@ -271,19 +308,23 @@
             remote(loc_lse.at[h, b], loc_lse_in.at[h, d], ls_s.at[h, d], ls_r.at[h, d], query_peer(h, d)),
         )
 
-    for d in (2, 1, 3, 0):
+    def local_step(i, carry):
+        d = lax.rem(i + 1, SIDE)
         for h in range(2):
             local_shard(h, d)
-            if d:
+
+        @pl.when(d != 0)
+        def _():
+            for h in range(2):
                 for cp in loc_out(h, d):
-                    go(cp)
-        if d == 2:
-            for h in range(2):
-                left, right = wrap(a_own[h] - 1), wrap(a_own[h] + 1)
-                mem_copy(h, 0, mem_buf.at[h, left, 0], 1).wait_recv()
-                go(mem_copy(h, 4, mem_buf.at[h, left, 0], 1))
-                mem_copy(h, 1, mem_buf.at[h, right, 1], 3).wait_recv()
-                go(mem_copy(h, 5, mem_buf.at[h, right, 1], 3))
+                    cp.start()
+
+        return carry
+
+    lax.fori_loop(0, 1, local_step, 0)
+    on(mem_rings, WAIT, 0, 1)
+    on(mem_rings, SEND, 4, 5)
+    lax.fori_loop(1, SIDE, local_step, 0)
 
     for h in range(2):
         for d in range(SIDE):
@@ -293,45 +334,39 @@
     to_smem = pltpu.make_async_copy(tab_buf, tab_sm, l_sem.at[count])
     to_smem.start()
     to_smem.wait()
-    for h in range(2):
-        left, right = wrap(a_own[h] - 1), wrap(a_own[h] + 1)
-        across = wrap(a_own[h] + 2)
-        mem_copy(h, 2, mem_buf.at[h, left, 1], 1).wait_recv()
-        mem_copy(h, 3, mem_buf.at[h, right, 0], 3).wait_recv()
-        mem_copy(h, 4, mem_buf.at[h, across, 0], 1).wait_recv()
-        mem_copy(h, 5, mem_buf.at[h, across, 1], 3).wait_recv()
+    on(mem_rings, WAIT, 2, 3, 4, 5)
+    for h in range(2):
         for d in range(SIDE):
             q_z_in(h, d).wait_recv()
 
     lane = lax.broadcasted_iota(jnp.int32, (1, 2 * MBLK), 1)
 
     def memory_shard(h, b, pz):
-        def block(blk, carry):
-            tok = pl.ds(pl.multiple_of(blk * QBLK, QBLK), QBLK)
-            q4 = q_buf[h, b, pz, :, tok, :].reshape(SHARE * QBLK, DH)
+        for blk in range(2):
+            tok = slice(blk * QBLK, (blk + 1) * QBLK)
             keys, vals, bias = [], [], []
             for a in range(SIDE):
                 shard = (a * 4 + y) * 2 + z if h == 0 else (x * 4 + a) * 2 + z
-                slots = [tab_sm[h, b, pz, blk, shard * 2 + k] for k in range(2)]
+                slots = [tab_sm[h, b, pz, 2 * blk + k, shard] for k in range(2)]
                 for slot in slots:
-                    at = jnp.maximum(slot, 0)
+                    at = jnp.clip(slot, 0, SHARD_BLOCKS - 1)
                     keys.append(mem_buf[h, a, 0, at])
                     vals.append(mem_buf[h, a, 1, at])
                 off = [jnp.where(slot < 0, NEG, 0.0) for slot in slots]
                 bias.append(jnp.where(lane < MBLK, off[0], off[1]))
-            s = dot_nt(q4, jnp.concatenate(keys, axis=0)) + jnp.concatenate(bias, axis=1)
-            top = jnp.max(s, axis=1, keepdims=True)
-            p = jnp.exp2((s - top) * FACTOR).astype(jnp.bfloat16)
-            both = jnp.dot(
-                p, with_ones(jnp.concatenate(vals, axis=0)), preferred_element_type=jnp.float32
-            )
-            total = both[:, DH:]
-            result = both[:, :DH] / total
-            mem_part[h, b, pz, :, tok, :] = result.astype(jnp.bfloat16).reshape(SHARE, QBLK, DH)
-            mem_lse[h, b, pz, :, tok] = rows_of(top * FACTOR + jnp.log2(total))
-            return carry
-
-        lax.fori_loop(0, 2, block, 0)
+            keys = jnp.concatenate(keys, axis=0)
+            vals = with_ones(jnp.concatenate(vals, axis=0))
+            bias = jnp.concatenate(bias, axis=1)
+            sums = []
+            for g in range(SHARE):
+                s = dot_nt(q_buf[h, b, pz, g, tok, :], keys) + bias
+                top = jnp.max(s, axis=1, keepdims=True)
+                p = jnp.exp2((s - top) * FACTOR).astype(jnp.bfloat16)
+                both = jnp.dot(p, vals, preferred_element_type=jnp.float32)
+                total = both[:, DH:]
+                mem_part[h, b, pz, g, tok, :] = (both[:, :DH] / total).astype(jnp.bfloat16)
+                sums.append(top * FACTOR + jnp.log2(total))
+            mem_lse[h, b, pz, :, tok] = rows_of(sums)
 
     def mem_out(h, part, d):
         b, pz = wrap(b_own[h] + d), (zo, z)[part]
@@ -355,13 +390,21 @@
         return total
 
     for part in range(2):
-        pz = (zo, z)[part]
-        for d in (2, 1, 3, 0):
+
+        def memory_step(i, carry, part=part):
+            d = lax.rem(i + 1, SIDE)
             for h in range(2):
-                memory_shard(h, wrap(b_own[h] + d), pz)
-                if d:
+                memory_shard(h, wrap(b_own[h] + d), (zo, z)[part])
+
+            @pl.when(d != 0)
+            def _():
+                for h in range(2):
                     for cp in mem_out(h, part, d):
-                        go(cp)
+                        cp.start()
+
+            return carry
+
+        lax.fori_loop(0, SIDE, memory_step, 0)
 
     for h in range(2):
         for d in range(1, SIDE):
@@ -403,16 +446,12 @@
                 go(z_data)
                 go(z_stat)
 
-    logits = jnp.zeros((ROWS, GROUPS * HEADS_DEV), jnp.float32)
+    logits = jnp.zeros((GROUPS * HEADS_DEV, ROWS), jnp.float32)
     for head in range(HEADS_DEV):
-        feats = pl.ds(head * DH, DH)
-        logits += jnp.dot(
-            loc_fin[head].astype(jnp.bfloat16), gw_ref[0, feats, :], preferred_element_type=jnp.float32
-        )
-        logits += jnp.dot(
-            mem_fin[head].astype(jnp.bfloat16), gw_ref[1, feats, :], preferred_element_type=jnp.float32
-        )
-    lg_out[...] = jnp.transpose(logits).reshape(GROUPS, HEADS_DEV, ROWS)
+        feats = slice(head * DH, (head + 1) * DH)
+        logits += dot_nt(gw_ref[0, :, feats], loc_fin[head].astype(jnp.bfloat16))
+        logits += dot_nt(gw_ref[1, :, feats], mem_fin[head].astype(jnp.bfloat16))
+    lg_out[...] = logits.reshape(GROUPS, HEADS_DEV, ROWS)
 
     def lg(d):
         to = lax.rem(g_own + d, GROUPS)
@@ -430,21 +469,12 @@
         mixed = share * mem_fin[head] + (1.0 - share) * loc_fin[head]
         out_ref[:, head * DH : (head + 1) * DH] = mixed.astype(jnp.bfloat16)
 
+    for h in range(2):
+        for d in range(1, SIDE):
+            for cp in loc_out(h, d) + mem_out(h, 0, d) + mem_out(h, 1, d):
+                cp.wait_send()
     for cp in started:
         cp.wait_send()
-
-
-def block_table(retrieval):
-    ids = retrieval.reshape(2, -1)
-    owner, offset = ids // SHARD_BLOCKS, ids % SHARD_BLOCKS
-    here = owner[:, None, :] == jnp.arange(32, dtype=jnp.int32)[None, :, None]
-    held = jnp.sum(here.astype(jnp.int32), axis=2)
-    low = jnp.min(jnp.where(here, offset[:, None, :], SHARD_BLOCKS), axis=2)
-    high = jnp.max(jnp.where(here, offset[:, None, :], -1), axis=2)
-    first = jnp.where(held > 0, low, -1)
-    second = jnp.where(held > 1, high, -1)
-    both = jnp.stack([first, second], axis=2).reshape(2, 64)
-    return jnp.pad(both, ((0, 6), (0, 64)))
 
 
 def on_device(queries, keys, values, mem_keys, mem_values, retrieval, gate_weight, gate_bias):
@@ -457,7 +487,7 @@
     return pl.pallas_call(
         kernel,
         out_shape=jax.ShapeDtypeStruct((ROWS, HEADS_DEV * DH), bf),
-        in_specs=[anywhere] * 6 + [vmem] * 2,
+        in_specs=[anywhere] * 5 + [vmem] * 3,
         out_specs=vmem,
         scratch_shapes=[
             pltpu.VMEM((2, SIDE, 2) + part, bf),
@@ -479,14 +509,14 @@
             pltpu.VMEM((2,) + stat, f32),
             pltpu.VMEM((HEADS_DEV, ROWS, DH), f32),
             pltpu.VMEM((HEADS_DEV, ROWS, DH), f32),
-            pltpu.VMEM((SHARE * QBLK, 2 * DH), f32),
-            pltpu.VMEM((SHARE * QBLK, DH), f32),
+            pltpu.VMEM((2 * SHARE, QBLK, 2 * DH), f32),
+            pltpu.VMEM((2 * SHARE, QBLK, DH), f32),
             pltpu.VMEM((GROUPS, HEADS_DEV, ROWS), f32),
             pltpu.VMEM((GROUPS, HEADS_DEV, ROWS), f32),
             dma((24,)),
             dma((2,)), dma((2,)),
-            dma((2, 2, SIDE)), dma((2, 2, SIDE)),
-            dma((2, SIDE)), dma((2, SIDE)),
+            dma((2, 2, 6)), dma((2, 2, 6)),
+            dma((2, 6)), dma((2, 6)),
             dma((2, SIDE)), dma((2, SIDE)),
             dma((2, 8)), dma((2, 8)),
             dma((2, 6)), dma((2, 6)),
@@ -502,8 +532,8 @@
             collective_id=0, has_side_effects=True, vmem_limit_bytes=60 * 2**20
         ),
     )(
-        queries, keys, values, mem_keys, mem_values, block_table(retrieval),
-        gate_weight, gate_bias.reshape(1, HEADS_DEV),
+        queries, keys, values, mem_keys, mem_values, retrieval.reshape(2, -1),
+        gate_weight.transpose(0, 2, 1), gate_bias.reshape(1, HEADS_DEV),
     )
 
 

time: 143 us -> 117 us (0.82)
  Pallas kernels: 137 us -> 114 us
  local copies, waits for them, and re-layouts: 5.26 us -> 1.87 us
    pallas_call x1, Pallas kernels: 137 us -> 114 us  [on_device(): pl.pallas_call(kernel, out_shape=jax.ShapeDtypeStruct((ROWS, HEADS_DEV *...]
    unnamed x4 -> x1, local copies, waits for them, and re-layouts: 4.45 us -> 1.87 us
where the time goes in v2:
time: 117 us; the launch traced here: 116 us
  Pallas kernels  114 us (97%)
  local copies, waits for them, and re-layouts  1.87 us (2%)
    pallas_call x1, Pallas kernels, on_device(): pl.pallas_call(kernel, out_shape=jax.ShapeDtypeStruct((ROWS, HEADS_DEV *...  114 us

profile of v2, /device:TPU:1, one launch (start us, length us, event | category | flops | bytes accessed | tf_op | source)
XLA Modules:
  0.0 116.3 jit_solution(9015165801387700471)
XLA Ops:
  0.0 114.4 %shard_map.82 = bf16[256,1024]{1,0:T(8,128)(2,1)} custom-call(bf16[256,1024]{1,0:T(8,128)(2,1)} %q_hbm.1, bf16[256,256]{1,0:T(8,128)(2,1)} %k_hbm.1, bf16[256,256]{1,0:T(8,128)(2,1)} %v_hbm.1, bf16[32,64,256]{2,1,0:T(8,128)(2,1)} %mk_hbm.1, bf16[32,64,256]{2,1,0:T(8,128)(2,1)} %mv_hbm.1, s32[2,32]{1,0:T(2,128)} %bitcast.4, bf16[2,32,1024]{2,1,0:T(8,128)(2,1)} %bitcast.3, ...), custom_call_target="tpu_custom_call" | custom-call | tf_op jit(solution)/shard_map/pallas_call | solution.py:487
  114.4 1.9 %copy.10 = bf16[256,1024]{1,0:T(8,128)(2,1)} copy(bf16[256,1024]{1,0:T(8,128)(2,1)} %shard_map.82) | data formatting | bytes 1048576

commit v3 on v2

--- a/solution.py
+++ b/solution.py
@@ -34,7 +34,7 @@
     shape = (QBLK, QBLK)
     eye = lax.broadcasted_iota(jnp.int32, shape, 0) == lax.broadcasted_iota(jnp.int32, shape, 1)
     rows = [jnp.sum(jnp.where(eye, piece, 0.0), axis=0, keepdims=True) for piece in pieces]
-    return jnp.concatenate(rows + [jnp.zeros((8 - SHARE, QBLK), jnp.float32)], axis=0)
+    return jnp.concatenate(rows + [jnp.zeros((6, QBLK), jnp.float32)], axis=0)
 
 
 def block_table(ids):
@@ -59,12 +59,10 @@
     q_hbm, k_hbm, v_hbm, mk_hbm, mv_hbm, ids_ref, gw_ref, gb_ref,
     out_ref,
     q_buf, kv_buf, mem_buf, tab_buf, tab_sm,
-    loc_part, loc_lse, loc_in, loc_lse_in,
-    mem_part, mem_lse, mem_in, mem_lse_in,
-    z_part, z_lse, z_in, z_lse_in,
+    part_buf, lse_buf, in_buf, in_lse, z_part, z_lse, z_in, z_lse_in,
     loc_fin, mem_fin, acc_ref, max_ref, lg_out, lg_in,
     l_sem, kvz_s, kvz_r, kva_s, kva_r, qb_s, qb_r, qz_s, qz_r, tab_s, tab_r, ma_s, ma_r,
-    lo_s, lo_r, ls_s, ls_r, me_s, me_r, ms_s, ms_r, z_s, z_r, zs_s, zs_r, lg_s, lg_r,
+    rs_s, rs_r, rl_s, rl_r, z_s, z_r, zs_s, zs_r, lg_s, lg_r,
 ):
     c = lax.axis_index("ctx")
     g_own = lax.axis_index("mem")
@@ -149,15 +147,21 @@
         out = [(own, 0, 1), (own, 1, 3), (own, 1, 1), (own, 0, 3), (left, 0, 1), (right, 1, 3)]
         come = [(left, 0), (right, 1), (left, 1), (right, 0), (across, 0), (across, 1)]
 
+        def copy(n):
+            at, half, d = out[n]
+            return remote(ref(at, half), ref(at, half), ssem.at[n], rsem.at[n], peer(h, d))
+
         def send(n):
-            at, half, d = out[n]
-            go(remote(ref(at, half), ref(at, half), ssem.at[n], rsem.at[n], peer(h, d)))
+            copy(n).start()
+
+        def sent(n):
+            copy(n).wait_send()
 
         def wait(n):
             at, half = come[n]
             remote(ref(at, half), ref(at, half), ssem.at[n], rsem.at[n], z_peer).wait_recv()
 
-        return send, wait
+        return send, wait, sent
 
     def kv_ring(h, part):
         pz = (z, zo)[part]
@@ -172,9 +176,11 @@
             qb_s.at[h], qb_r.at[h],
         )
 
-    def mem_ring(h):
+    def mem_ring(h, part):
+        blocks = pl.ds(part * (SHARD_BLOCKS // 2), SHARD_BLOCKS // 2)
         return ring(
-            h, a_own[h], key_peer, lambda at, half: mem_buf.at[h, at, half], ma_s.at[h], ma_r.at[h]
+            h, a_own[h], key_peer, lambda at, half: mem_buf.at[h, at, half, blocks],
+            ma_s.at[h, part], ma_r.at[h, part],
         )
 
     def q_z(h, d):
@@ -202,14 +208,15 @@
     q_rings = [q_ring(h) for h in range(2)]
     kv_rings = [kv_ring(h, 0) for h in range(2)]
     kvo_rings = [kv_ring(h, 1) for h in range(2)]
-    mem_rings = [mem_ring(h) for h in range(2)]
+    mem_a_rings = [mem_ring(h, 0) for h in range(2)]
+    mem_b_rings = [mem_ring(h, 1) for h in range(2)]
 
     def on(rings, what, *steps):
         for n in steps:
             for r in rings:
                 r[what](n)
 
-    SEND, WAIT = 0, 1
+    SEND, WAIT, SENT = 0, 1, 2
     for cp in kv_local:
         cp.wait()
     for h in range(2):
@@ -224,7 +231,22 @@
         go(q_z(h, 0))
     for cp in mem_local:
         cp.wait()
-    on(mem_rings, SEND, 0, 1)
+    on(mem_a_rings, SEND, 0, 1)
+    for h in range(2):
+        kv_z_in(h).wait_recv()
+    on(kvo_rings, SEND, 0, 1, 2, 3)
+    on(q_rings, WAIT, 0, 1)
+    on(q_rings, SEND, 4, 5)
+    on(kv_rings, WAIT, 0, 1)
+    on(kv_rings, SEND, 4, 5)
+    on(mem_a_rings, SEND, 2, 3)
+    on(q_rings, WAIT, 2, 3)
+    for h in range(2):
+        go(q_z(h, 1))
+        go(q_z(h, 3))
+    on(kvo_rings, WAIT, 0, 1)
+    on(kvo_rings, SEND, 4, 5)
+    on(mem_b_rings, SEND, 0, 1, 2, 3)
     for h in range(2):
         tab_buf[h, b_own[h], z] = block_table(ids_ref[...])
     for h in range(2):
@@ -232,26 +254,13 @@
             for dz in range(2):
                 if d or dz:
                     go(tab(h, d, dz))
-
-    on(q_rings, WAIT, 0, 1)
-    on(q_rings, SEND, 4, 5)
-    on(kv_rings, WAIT, 0, 1)
-    on(kv_rings, SEND, 4, 5)
-    for h in range(2):
-        kv_z_in(h).wait_recv()
-    on(kvo_rings, SEND, 0, 1, 2, 3)
-    on(mem_rings, SEND, 2, 3)
-    on(q_rings, WAIT, 2, 3)
-    for h in range(2):
-        go(q_z(h, 1))
-        go(q_z(h, 3))
-    on(kvo_rings, WAIT, 0, 1)
-    on(kvo_rings, SEND, 4, 5)
     on(q_rings, WAIT, 4, 5)
     for h in range(2):
         go(q_z(h, 2))
     on(kv_rings, WAIT, 2, 3, 4, 5)
     on(kvo_rings, WAIT, 2, 3, 4, 5)
+    on(mem_a_rings, WAIT, 0, 1)
+    on(mem_a_rings, SEND, 4, 5)
 
     def local_shard(h, d):
         b = wrap(b_own[h] + d)
@@ -297,34 +306,92 @@
                 total = acc_ref[n, :, DH:]
                 some = total > 0.0
                 safe = jnp.where(some, total, 1.0)
-                loc_part[h, b, g, tok, :] = (acc_ref[n, :, :DH] / safe).astype(jnp.bfloat16)
+                part_buf[0, h, b, g, tok, :] = (acc_ref[n, :, :DH] / safe).astype(jnp.bfloat16)
                 sums.append(jnp.where(some, max_ref[n] * FACTOR + jnp.log2(safe), NEG))
-            loc_lse[h, b, :, tok] = rows_of(sums)
-
-    def loc_out(h, d):
-        b = wrap(b_own[h] + d)
+            lse_buf[0, h, b, 0, :, tok] = rows_of(sums[:2])
+            lse_buf[0, h, b, 1, :, tok] = rows_of(sums[2:])
+
+    MESSAGES = [(2, 0, 1, 0), (2, 1, 3, 0), (1, 1, 1, 1), (3, 0, 3, 2), (1, 0, 1, 1), (3, 1, 3, 2)]
+
+    def result_copies(job, h, n):
+        whose, half, way, lands = MESSAGES[n]
+        b = wrap(b_own[h] + whose)
+        heads = pl.ds(2 * half, 2)
+        peer = query_peer(h, way)
         return (
-            remote(loc_part.at[h, b], loc_in.at[h, d], lo_s.at[h, d], lo_r.at[h, d], query_peer(h, d)),
-            remote(loc_lse.at[h, b], loc_lse_in.at[h, d], ls_s.at[h, d], ls_r.at[h, d], query_peer(h, d)),
+            remote(
+                part_buf.at[job, h, b, heads], in_buf.at[job, h, lands, heads],
+                rs_s.at[job, h, n], rs_r.at[job, h, n], peer,
+            ),
+            remote(
+                lse_buf.at[job, h, b, half], in_lse.at[job, h, lands, half],
+                rl_s.at[job, h, n], rl_r.at[job, h, n], peer,
+            ),
         )
 
+    def send_results(job, *numbers, hs=(0, 1)):
+        for n in numbers:
+            for h in hs:
+                for cp in result_copies(job, h, n):
+                    cp.start()
+
+    def await_results(job, *numbers, hs=(0, 1)):
+        for n in numbers:
+            for h in hs:
+                for cp in result_copies(job, h, n):
+                    cp.wait_recv()
+
+    def weights(stats):
+        top = functools.reduce(jnp.maximum, stats)
+        powers = [jnp.exp2(s - top) for s in stats]
+        total = functools.reduce(jnp.add, powers)
+        scales = [jnp.transpose(p / total) for p in powers]
+        return scales, top + jnp.log2(total)
+
+    def merge(parts, scales, g):
+        total = None
+        for part, scale in zip(parts, scales):
+            term = part[g].astype(jnp.float32) * scale[:, g % 2 : g % 2 + 1]
+            total = term if total is None else total + term
+        return total
+
+    def pass_on(job):
+        for half in range(2):
+            for h in range(2):
+                await_results(job, half, hs=(h,))
+                b = wrap(b_own[h] + (1, 3)[half])
+                mine, other = part_buf.at[job, h, b], in_buf.at[job, h, 0]
+                scales, whole = weights([lse_buf[job, h, b, half], in_lse[job, h, 0, half]])
+                for g in (2 * half, 2 * half + 1):
+                    mine[g] = merge([mine, other], scales, g).astype(jnp.bfloat16)
+                lse_buf[job, h, b, half] = whole
+                send_results(job, 4 + half, hs=(h,))
+
+    def finish(job, h, half, more_parts=(), more_stats=()):
+        b = b_own[h]
+        await_results(job, *((3, 4), (2, 5))[half], hs=(h,))
+        parts = [part_buf.at[job, h, b], in_buf.at[job, h, 1], in_buf.at[job, h, 2], *more_parts]
+        stats = [lse_buf[job, h, b, half], in_lse[job, h, 1, half], in_lse[job, h, 2, half], *more_stats]
+        scales, whole = weights(stats)
+        return [merge(parts, scales, g) for g in (2 * half, 2 * half + 1)], whole
+
+    def order(i):
+        return jnp.where(i == 0, 2, jnp.where(i == 1, 1, jnp.where(i == 2, 3, 0)))
+
     def local_step(i, carry):
-        d = lax.rem(i + 1, SIDE)
         for h in range(2):
-            local_shard(h, d)
-
-        @pl.when(d != 0)
+            local_shard(h, order(i))
+        @pl.when(i == 0)
         def _():
-            for h in range(2):
-                for cp in loc_out(h, d):
-                    cp.start()
-
+            send_results(0, 0, 1)
+            on(mem_b_rings, WAIT, 0, 1)
+            on(mem_b_rings, SEND, 4, 5)
+
+        pl.when(i == 1)(lambda: send_results(0, 2))
+        pl.when(i == 2)(lambda: send_results(0, 3))
         return carry
 
-    lax.fori_loop(0, 1, local_step, 0)
-    on(mem_rings, WAIT, 0, 1)
-    on(mem_rings, SEND, 4, 5)
-    lax.fori_loop(1, SIDE, local_step, 0)
+    lax.fori_loop(0, SIDE, local_step, 0)
 
     for h in range(2):
         for d in range(SIDE):
@@ -334,14 +401,16 @@
     to_smem = pltpu.make_async_copy(tab_buf, tab_sm, l_sem.at[count])
     to_smem.start()
     to_smem.wait()
-    on(mem_rings, WAIT, 2, 3, 4, 5)
+    pass_on(0)
+    on(mem_a_rings, WAIT, 2, 3, 4, 5)
+    on(mem_b_rings, WAIT, 2, 3, 4, 5)
     for h in range(2):
         for d in range(SIDE):
             q_z_in(h, d).wait_recv()
 
     lane = lax.broadcasted_iota(jnp.int32, (1, 2 * MBLK), 1)
 
-    def memory_shard(h, b, pz):
+    def memory_shard(job, h, b, pz):
         for blk in range(2):
             tok = slice(blk * QBLK, (blk + 1) * QBLK)
             keys, vals, bias = [], [], []
@@ -364,93 +433,67 @@
                 p = jnp.exp2((s - top) * FACTOR).astype(jnp.bfloat16)
                 both = jnp.dot(p, vals, preferred_element_type=jnp.float32)
                 total = both[:, DH:]
-                mem_part[h, b, pz, g, tok, :] = (both[:, :DH] / total).astype(jnp.bfloat16)
+                part_buf[job, h, b, g, tok, :] = (both[:, :DH] / total).astype(jnp.bfloat16)
                 sums.append(top * FACTOR + jnp.log2(total))
-            mem_lse[h, b, pz, :, tok] = rows_of(sums)
-
-    def mem_out(h, part, d):
-        b, pz = wrap(b_own[h] + d), (zo, z)[part]
+            lse_buf[job, h, b, 0, :, tok] = rows_of(sums[:2])
+            lse_buf[job, h, b, 1, :, tok] = rows_of(sums[2:])
+
+    def z_copies(h, half):
+        heads = pl.ds(2 * half, 2)
+        n = 2 * h + half
         return (
-            remote(mem_part.at[h, b, pz], mem_in.at[h, part, d], me_s.at[h, part, d], me_r.at[h, part, d], query_peer(h, d)),
-            remote(mem_lse.at[h, b, pz], mem_lse_in.at[h, part, d], ms_s.at[h, part, d], ms_r.at[h, part, d], query_peer(h, d)),
+            remote(z_part.at[h, heads], z_in.at[h, heads], z_s.at[n], z_r.at[n], z_peer),
+            remote(z_lse.at[h, half], z_lse_in.at[h, half], zs_s.at[n], zs_r.at[n], z_peer),
         )
 
-    def weights(stats):
-        top = functools.reduce(jnp.maximum, stats)
-        powers = [jnp.exp2(s - top) for s in stats]
-        total = functools.reduce(jnp.add, powers)
-        scales = [jnp.transpose(p / total) for p in powers]
-        return scales, top + jnp.log2(total)
-
-    def merge(parts, scales, g):
-        total = None
-        for part, scale in zip(parts, scales):
-            term = part(g).astype(jnp.float32) * scale[:, g : g + 1]
-            total = term if total is None else total + term
-        return total
-
-    for part in range(2):
-
-        def memory_step(i, carry, part=part):
-            d = lax.rem(i + 1, SIDE)
+    def to_z_peer():
+        for half in range(2):
             for h in range(2):
-                memory_shard(h, wrap(b_own[h] + d), (zo, z)[part])
-
-            @pl.when(d != 0)
-            def _():
-                for h in range(2):
-                    for cp in mem_out(h, part, d):
-                        cp.start()
-
-            return carry
-
-        lax.fori_loop(0, SIDE, memory_step, 0)
-
-    for h in range(2):
-        for d in range(1, SIDE):
-            for cp in loc_out(h, d):
+                results, whole = finish(1, h, half)
+                for k in range(2):
+                    z_part[h, 2 * half + k] = results[k].astype(jnp.bfloat16)
+                z_lse[h, half] = whole
+                for cp in z_copies(h, half):
+                    cp.start()
+
+    def memory_step(i, carry):
+        job = 1 + i // SIDE
+        for h in range(2):
+            memory_shard(job, h, wrap(b_own[h] + order(i % SIDE)), jnp.where(job == 1, zo, z))
+        pl.when(i == 0)(lambda: send_results(1, 0, 1))
+        pl.when(i == 1)(lambda: send_results(1, 2))
+        pl.when(i == 2)(lambda: send_results(1, 3))
+        pl.when(i == 3)(lambda: pass_on(1))
+        pl.when(i == 4)(lambda: send_results(2, 0, 1))
+        pl.when(i == 5)(lambda: send_results(2, 2))
+        pl.when(i == 5)(to_z_peer)
+        pl.when(i == 6)(lambda: send_results(2, 3))
+        pl.when(i == 7)(lambda: pass_on(2))
+        return carry
+
+    lax.fori_loop(0, 2 * SIDE, memory_step, 0)
+
+    def gate_dot(which, fin, head):
+        feats = slice(head * DH, (head + 1) * DH)
+        return dot_nt(gw_ref[which, :, feats], fin[head].astype(jnp.bfloat16))
+
+    logits = jnp.zeros((GROUPS * HEADS_DEV, ROWS), jnp.float32)
+    for half in range(2):
+        for h in range(2):
+            results, _ = finish(0, h, half)
+            for k in range(2):
+                head = h * SHARE + 2 * half + k
+                loc_fin[head] = results[k]
+                logits += gate_dot(0, loc_fin, head)
+    for half in range(2):
+        for h in range(2):
+            for cp in z_copies(h, half):
                 cp.wait_recv()
-        stats = [loc_lse[h, b_own[h]]] + [loc_lse_in[h, d] for d in range(1, SIDE)]
-        scales, _ = weights(stats)
-        parts = [lambda g, h=h: loc_part[h, b_own[h], g]]
-        parts += [lambda g, h=h, d=d: loc_in[h, d, g] for d in range(1, SIDE)]
-        for g in range(SHARE):
-            loc_fin[h * SHARE + g] = merge(parts, scales, g)
-
-    for part in range(2):
-        pz = (zo, z)[part]
-        for h in range(2):
-            for d in range(1, SIDE):
-                for cp in mem_out(h, part, d):
-                    cp.wait_recv()
-            stats = [mem_lse[h, b_own[h], pz]]
-            stats += [mem_lse_in[h, part, d] for d in range(1, SIDE)]
-            parts = [lambda g, h=h, pz=pz: mem_part[h, b_own[h], pz, g]]
-            parts += [lambda g, h=h, d=d, part=part: mem_in[h, part, d, g] for d in range(1, SIDE)]
-            z_data = remote(z_part.at[h], z_in.at[h], z_s.at[h], z_r.at[h], z_peer)
-            z_stat = remote(z_lse.at[h], z_lse_in.at[h], zs_s.at[h], zs_r.at[h], z_peer)
-            if part == 1:
-                z_data.wait_recv()
-                z_stat.wait_recv()
-                stats.append(z_lse_in[h])
-                parts.append(lambda g, h=h: z_in[h, g])
-            scales, whole = weights(stats)
-            for g in range(SHARE):
-                result = merge(parts, scales, g)
-                if part == 0:
-                    z_part[h, g] = result.astype(jnp.bfloat16)
-                else:
-                    mem_fin[h * SHARE + g] = result
-            if part == 0:
-                z_lse[h] = whole
-                go(z_data)
-                go(z_stat)
-
-    logits = jnp.zeros((GROUPS * HEADS_DEV, ROWS), jnp.float32)
-    for head in range(HEADS_DEV):
-        feats = slice(head * DH, (head + 1) * DH)
-        logits += dot_nt(gw_ref[0, :, feats], loc_fin[head].astype(jnp.bfloat16))
-        logits += dot_nt(gw_ref[1, :, feats], mem_fin[head].astype(jnp.bfloat16))
+            results, _ = finish(2, h, half, [z_in.at[h]], [z_lse_in[h, half]])
+            for k in range(2):
+                head = h * SHARE + 2 * half + k
+                mem_fin[head] = results[k]
+                logits += gate_dot(1, mem_fin, head)
     lg_out[...] = logits.reshape(GROUPS, HEADS_DEV, ROWS)
 
     def lg(d):
@@ -470,9 +513,15 @@
         out_ref[:, head * DH : (head + 1) * DH] = mixed.astype(jnp.bfloat16)
 
     for h in range(2):
-        for d in range(1, SIDE):
-            for cp in loc_out(h, d) + mem_out(h, 0, d) + mem_out(h, 1, d):
+        for job in range(3):
+            for n in range(6):
+                for cp in result_copies(job, h, n):
+                    cp.wait_send()
+        for half in range(2):
+            for cp in z_copies(h, half):
                 cp.wait_send()
+    for rings in (q_rings, kv_rings, kvo_rings, mem_a_rings, mem_b_rings):
+        on(rings, SENT, *range(6))
     for cp in started:
         cp.wait_send()
 
@@ -495,18 +544,14 @@
             pltpu.VMEM((2, SIDE, 2, SHARD_BLOCKS, MBLK, DH), bf),
             pltpu.VMEM((2, SIDE, 2, 8, 128), jnp.int32),
             pltpu.SMEM((2, SIDE, 2, 8, 128), jnp.int32),
-            pltpu.VMEM((2, SIDE) + part, bf),
-            pltpu.VMEM((2, SIDE) + stat, f32),
-            pltpu.VMEM((2, SIDE) + part, bf),
-            pltpu.VMEM((2, SIDE) + stat, f32),
-            pltpu.VMEM((2, SIDE, 2) + part, bf),
-            pltpu.VMEM((2, SIDE, 2) + stat, f32),
-            pltpu.VMEM((2, 2, SIDE) + part, bf),
-            pltpu.VMEM((2, 2, SIDE) + stat, f32),
+            pltpu.VMEM((3, 2, SIDE) + part, bf),
+            pltpu.VMEM((3, 2, SIDE, 2) + stat, f32),
+            pltpu.VMEM((3, 2, 3) + part, bf),
+            pltpu.VMEM((3, 2, 3, 2) + stat, f32),
             pltpu.VMEM((2,) + part, bf),
-            pltpu.VMEM((2,) + stat, f32),
+            pltpu.VMEM((2, 2) + stat, f32),
             pltpu.VMEM((2,) + part, bf),
-            pltpu.VMEM((2,) + stat, f32),
+            pltpu.VMEM((2, 2) + stat, f32),
             pltpu.VMEM((HEADS_DEV, ROWS, DH), f32),
             pltpu.VMEM((HEADS_DEV, ROWS, DH), f32),
             pltpu.VMEM((2 * SHARE, QBLK, 2 * DH), f32),
@@ -519,13 +564,11 @@
             dma((2, 6)), dma((2, 6)),
             dma((2, SIDE)), dma((2, SIDE)),
             dma((2, 8)), dma((2, 8)),
-            dma((2, 6)), dma((2, 6)),
-            dma((2, SIDE)), dma((2, SIDE)),
-            dma((2, SIDE)), dma((2, SIDE)),
-            dma((2, 2, SIDE)), dma((2, 2, SIDE)),
-            dma((2, 2, SIDE)), dma((2, 2, SIDE)),
-            dma((2,)), dma((2,)),
-            dma((2,)), dma((2,)),
+            dma((2, 2, 6)), dma((2, 2, 6)),
+            dma((3, 2, 6)), dma((3, 2, 6)),
+            dma((3, 2, 6)), dma((3, 2, 6)),
+            dma((4,)), dma((4,)),
+            dma((4,)), dma((4,)),
             dma((SIDE,)), dma((SIDE,)),
         ],
         compiler_params=pltpu.CompilerParams(

time: 117 us -> 104 us (0.89)
  Pallas kernels: 114 us -> 102 us
    pallas_call x1, Pallas kernels: 114 us -> 102 us  [on_device(): pl.pallas_call(kernel, out_shape=jax.ShapeDtypeStruct((ROWS, HEADS_DEV *...]
where the time goes in v3:
time: 104 us
  Pallas kernels  102 us (98%)
  local copies, waits for them, and re-layouts  1.87 us (2%)
    pallas_call x1, Pallas kernels, on_device(): pl.pallas_call(kernel, out_shape=jax.ShapeDtypeStruct((ROWS, HEADS_DEV *...  102 us

profile of v3, /device:TPU:1, one launch (start us, length us, event | category | flops | bytes accessed | tf_op | source)
XLA Modules:
  0.0 103.7 jit_solution(9301535055587172580)
XLA Ops:
  0.0 101.8 %shard_map.82 = bf16[256,1024]{1,0:T(8,128)(2,1)} custom-call(bf16[256,1024]{1,0:T(8,128)(2,1)} %q_hbm.1, bf16[256,256]{1,0:T(8,128)(2,1)} %k_hbm.1, bf16[256,256]{1,0:T(8,128)(2,1)} %v_hbm.1, bf16[32,64,256]{2,1,0:T(8,128)(2,1)} %mk_hbm.1, bf16[32,64,256]{2,1,0:T(8,128)(2,1)} %mv_hbm.1, s32[2,32]{1,0:T(2,128)} %bitcast.4, bf16[2,32,1024]{2,1,0:T(8,128)(2,1)} %bitcast.3, ...), custom_call_target="tpu_custom_call" | custom-call | tf_op jit(solution)/shard_map/pallas_call | solution.py:536
  101.9 1.9 %copy.10 = bf16[256,1024]{1,0:T(8,128)(2,1)} copy(bf16[256,1024]{1,0:T(8,128)(2,1)} %shard_map.82) | data formatting | bytes 1048576

commit v4 on v3

--- a/solution.py
+++ b/solution.py
@@ -56,11 +56,11 @@
 
 
 def kernel(
-    q_hbm, k_hbm, v_hbm, mk_hbm, mv_hbm, ids_ref, gw_ref, gb_ref,
+    q_hbm, k_hbm, v_hbm, mk_hbm, mv_hbm, ids_hbm, gw_hbm, gb_hbm,
     out_ref,
     q_buf, kv_buf, mem_buf, tab_buf, tab_sm,
     part_buf, lse_buf, in_buf, in_lse, z_part, z_lse, z_in, z_lse_in,
-    loc_fin, mem_fin, acc_ref, max_ref, lg_out, lg_in,
+    loc_fin, mem_fin, acc_ref, max_ref, lg_out, lg_in, ids_ref, gw_ref, gb_ref,
     l_sem, kvz_s, kvz_r, kva_s, kva_r, qb_s, qb_r, qz_s, qz_r, tab_s, tab_r, ma_s, ma_r,
     rs_s, rs_r, rl_s, rl_r, z_s, z_r, zs_s, zs_r, lg_s, lg_r,
 ):
@@ -79,7 +79,13 @@
         return device(wrap(x + d), y, z) if h == 0 else device(x, wrap(y + d), z)
 
     def query_peer(h, d):
-        return key_peer(1 - h, d)
+        if isinstance(h, int):
+            return key_peer(1 - h, d)
+        px = jnp.where(h == 0, x, wrap(x + d))
+        return device(px, jnp.where(h == 0, wrap(y + d), y), z)
+
+    def query_own(h):
+        return b_own[h] if isinstance(h, int) else jnp.where(h == 0, y, x)
 
     z_peer = device(x, y, zo)
     a_own = (x, y)
@@ -91,7 +97,7 @@
             device_id=peer, device_id_type=MESH,
         )
 
-    kv_local, q_local, mem_local = [], [], []
+    kv_local, q_local, mem_local, small_local = [], [], [], []
     count = 0
 
     def local(src, dst, group):
@@ -117,11 +123,15 @@
         local(mk_hbm.at[:, :, cols], mem_buf.at[h, a_own[h], 0], mem_local)
         local(mv_hbm.at[:, :, cols], mem_buf.at[h, a_own[h], 1], mem_local)
 
+    local(ids_hbm, ids_ref, small_local)
+    local(gw_hbm, gw_ref, small_local)
+    local(gb_hbm, gb_ref, small_local)
+
     barrier = pltpu.get_barrier_semaphore()
     greeted = [z_peer]
-    for d in range(1, SIDE):
+    for d in (1, 3):
         greeted += [device(wrap(x + d), y, z), device(x, wrap(y + d), z)]
-        greeted += [device(wrap(x + d), y, zo), device(x, wrap(y + d), zo)]
+    for d in range(1, GROUPS):
         greeted += [(c, lax.rem(g_own + d, GROUPS))]
     for peer in greeted:
         pl.semaphore_signal(barrier, inc=1, device_id=peer, device_id_type=MESH)
@@ -191,19 +201,19 @@
         ref = q_buf.at[h, wrap(b_own[h] + d), zo]
         return remote(ref, ref, qz_s.at[h, d], qz_r.at[h, d], z_peer)
 
-    def tab_peer(h, d, dz):
-        pz = zo if dz else z
-        return device(x, wrap(y + d), pz) if h == 0 else device(wrap(x + d), y, pz)
-
-    def tab(h, d, dz):
-        ref = tab_buf.at[h, b_own[h], z]
-        sem = d * 2 + dz
-        return remote(ref, ref, tab_s.at[h, sem], tab_r.at[h, sem], tab_peer(h, d, dz))
-
-    def tab_in(h, d, dz):
-        ref = tab_buf.at[h, wrap(b_own[h] - d), zo if dz else z]
-        sem = d * 2 + dz
-        return remote(ref, ref, tab_s.at[h, sem], tab_r.at[h, sem], tab_peer(h, d, dz))
+    def tab(h, n, at, pz, peer):
+        ref = tab_buf.at[h, wrap(b_own[h] + at), pz]
+        return remote(ref, ref, tab_s.at[h, n], tab_r.at[h, n], peer)
+
+    def tab_out(h, n):
+        at, way = ((0, 1), (0, 3), (-1, 1))[n]
+        return tab(h, n, at, z, query_peer(h, way))
+
+    def tab_in(h, n):
+        return tab(h, n, (-1, 1, 2)[n], z, z_peer)
+
+    def tab_z(h, d, pz):
+        return tab(h, 3 + d, d, pz, z_peer)
 
     q_rings = [q_ring(h) for h in range(2)]
     kv_rings = [kv_ring(h, 0) for h in range(2)]
@@ -232,6 +242,14 @@
     for cp in mem_local:
         cp.wait()
     on(mem_a_rings, SEND, 0, 1)
+    for cp in small_local:
+        cp.wait()
+    for h in range(2):
+        tab_buf[h, b_own[h], z] = block_table(ids_ref[...])
+    for h in range(2):
+        go(tab_out(h, 0))
+        go(tab_out(h, 1))
+        go(tab_z(h, 0, z))
     for h in range(2):
         kv_z_in(h).wait_recv()
     on(kvo_rings, SEND, 0, 1, 2, 3)
@@ -246,19 +264,21 @@
         go(q_z(h, 3))
     on(kvo_rings, WAIT, 0, 1)
     on(kvo_rings, SEND, 4, 5)
+    for h in range(2):
+        tab_in(h, 0).wait_recv()
+        tab_in(h, 1).wait_recv()
+        go(tab_out(h, 2))
+        go(tab_z(h, 3, z))
+        go(tab_z(h, 1, z))
     on(mem_b_rings, SEND, 0, 1, 2, 3)
-    for h in range(2):
-        tab_buf[h, b_own[h], z] = block_table(ids_ref[...])
-    for h in range(2):
-        for d in range(SIDE):
-            for dz in range(2):
-                if d or dz:
-                    go(tab(h, d, dz))
     on(q_rings, WAIT, 4, 5)
     for h in range(2):
         go(q_z(h, 2))
     on(kv_rings, WAIT, 2, 3, 4, 5)
     on(kvo_rings, WAIT, 2, 3, 4, 5)
+    for h in range(2):
+        tab_in(h, 2).wait_recv()
+        go(tab_z(h, 2, z))
     on(mem_a_rings, WAIT, 0, 1)
     on(mem_a_rings, SEND, 4, 5)
 
@@ -313,9 +333,8 @@
 
     MESSAGES = [(2, 0, 1, 0), (2, 1, 3, 0), (1, 1, 1, 1), (3, 0, 3, 2), (1, 0, 1, 1), (3, 1, 3, 2)]
 
-    def result_copies(job, h, n):
-        whose, half, way, lands = MESSAGES[n]
-        b = wrap(b_own[h] + whose)
+    def result_copies(job, h, n, whose, half, way, lands):
+        b = wrap(query_own(h) + whose)
         heads = pl.ds(2 * half, 2)
         peer = query_peer(h, way)
         return (
@@ -329,17 +348,16 @@
             ),
         )
 
-    def send_results(job, *numbers, hs=(0, 1)):
+    def send_results(job, *numbers):
         for n in numbers:
-            for h in hs:
-                for cp in result_copies(job, h, n):
+            for h in range(2):
+                for cp in result_copies(job, h, n, *MESSAGES[n]):
                     cp.start()
 
-    def await_results(job, *numbers, hs=(0, 1)):
-        for n in numbers:
-            for h in hs:
-                for cp in result_copies(job, h, n):
-                    cp.wait_recv()
+    def each_pair(body, init=0):
+        for m in range(4):
+            init = body(m % 2, m // 2, init)
+        return init
 
     def weights(stats):
         top = functools.reduce(jnp.maximum, stats)
@@ -348,32 +366,40 @@
         scales = [jnp.transpose(p / total) for p in powers]
         return scales, top + jnp.log2(total)
 
-    def merge(parts, scales, g):
+    def merge(parts, scales, half, k):
         total = None
         for part, scale in zip(parts, scales):
-            term = part[g].astype(jnp.float32) * scale[:, g % 2 : g % 2 + 1]
+            term = part[2 * half + k].astype(jnp.float32) * scale[:, k : k + 1]
             total = term if total is None else total + term
         return total
 
     def pass_on(job):
-        for half in range(2):
-            for h in range(2):
-                await_results(job, half, hs=(h,))
-                b = wrap(b_own[h] + (1, 3)[half])
-                mine, other = part_buf.at[job, h, b], in_buf.at[job, h, 0]
-                scales, whole = weights([lse_buf[job, h, b, half], in_lse[job, h, 0, half]])
-                for g in (2 * half, 2 * half + 1):
-                    mine[g] = merge([mine, other], scales, g).astype(jnp.bfloat16)
-                lse_buf[job, h, b, half] = whole
-                send_results(job, 4 + half, hs=(h,))
+        def pair(h, half, carry):
+            way = 1 + 2 * half
+            for cp in result_copies(job, h, half, 2, half, way, 0):
+                cp.wait_recv()
+            b = wrap(query_own(h) + way)
+            mine, other = part_buf.at[job, h, b], in_buf.at[job, h, 0]
+            scales, whole = weights([lse_buf[job, h, b, half], in_lse[job, h, 0, half]])
+            for k in range(2):
+                mine[2 * half + k] = merge([mine, other], scales, half, k).astype(jnp.bfloat16)
+            lse_buf[job, h, b, half] = whole
+            for cp in result_copies(job, h, 4 + half, way, half, way, 1 + half):
+                cp.start()
+            return carry
+
+        each_pair(pair)
 
     def finish(job, h, half, more_parts=(), more_stats=()):
-        b = b_own[h]
-        await_results(job, *((3, 4), (2, 5))[half], hs=(h,))
+        b = query_own(h)
+        left, right = jnp.where(half == 0, 4, 2), jnp.where(half == 0, 3, 5)
+        for n, lands in ((left, 1), (right, 2)):
+            for cp in result_copies(job, h, n, 0, half, 1, lands):
+                cp.wait_recv()
         parts = [part_buf.at[job, h, b], in_buf.at[job, h, 1], in_buf.at[job, h, 2], *more_parts]
         stats = [lse_buf[job, h, b, half], in_lse[job, h, 1, half], in_lse[job, h, 2, half], *more_stats]
         scales, whole = weights(stats)
-        return [merge(parts, scales, g) for g in (2 * half, 2 * half + 1)], whole
+        return [merge(parts, scales, half, k) for k in range(2)], whole
 
     def order(i):
         return jnp.where(i == 0, 2, jnp.where(i == 1, 1, jnp.where(i == 2, 3, 0)))
@@ -395,13 +421,10 @@
 
     for h in range(2):
         for d in range(SIDE):
-            for dz in range(2):
-                if d or dz:
-                    tab_in(h, d, dz).wait_recv()
+            tab_z(h, d, zo).wait_recv()
     to_smem = pltpu.make_async_copy(tab_buf, tab_sm, l_sem.at[count])
     to_smem.start()
     to_smem.wait()
-    pass_on(0)
     on(mem_a_rings, WAIT, 2, 3, 4, 5)
     on(mem_b_rings, WAIT, 2, 3, 4, 5)
     for h in range(2):
@@ -447,14 +470,16 @@
         )
 
     def to_z_peer():
-        for half in range(2):
-            for h in range(2):
-                results, whole = finish(1, h, half)
-                for k in range(2):
-                    z_part[h, 2 * half + k] = results[k].astype(jnp.bfloat16)
-                z_lse[h, half] = whole
-                for cp in z_copies(h, half):
-                    cp.start()
+        def pair(h, half, carry):
+            results, whole = finish(1, h, half)
+            for k in range(2):
+                z_part[h, 2 * half + k] = results[k].astype(jnp.bfloat16)
+            z_lse[h, half] = whole
+            for cp in z_copies(h, half):
+                cp.start()
+            return carry
+
+        each_pair(pair)
 
     def memory_step(i, carry):
         job = 1 + i // SIDE
@@ -465,6 +490,7 @@
         pl.when(i == 2)(lambda: send_results(1, 3))
         pl.when(i == 3)(lambda: pass_on(1))
         pl.when(i == 4)(lambda: send_results(2, 0, 1))
+        pl.when(i == 4)(lambda: pass_on(0))
         pl.when(i == 5)(lambda: send_results(2, 2))
         pl.when(i == 5)(to_z_peer)
         pl.when(i == 6)(lambda: send_results(2, 3))
@@ -474,26 +500,29 @@
     lax.fori_loop(0, 2 * SIDE, memory_step, 0)
 
     def gate_dot(which, fin, head):
-        feats = slice(head * DH, (head + 1) * DH)
+        feats = pl.ds(pl.multiple_of(head * DH, DH), DH)
         return dot_nt(gw_ref[which, :, feats], fin[head].astype(jnp.bfloat16))
 
-    logits = jnp.zeros((GROUPS * HEADS_DEV, ROWS), jnp.float32)
-    for half in range(2):
-        for h in range(2):
-            results, _ = finish(0, h, half)
-            for k in range(2):
-                head = h * SHARE + 2 * half + k
-                loc_fin[head] = results[k]
-                logits += gate_dot(0, loc_fin, head)
-    for half in range(2):
-        for h in range(2):
-            for cp in z_copies(h, half):
-                cp.wait_recv()
-            results, _ = finish(2, h, half, [z_in.at[h]], [z_lse_in[h, half]])
-            for k in range(2):
-                head = h * SHARE + 2 * half + k
-                mem_fin[head] = results[k]
-                logits += gate_dot(1, mem_fin, head)
+    def local_pair(h, half, logits):
+        results, _ = finish(0, h, half)
+        for k in range(2):
+            head = h * SHARE + 2 * half + k
+            loc_fin[head] = results[k]
+            logits += gate_dot(0, loc_fin, head)
+        return logits
+
+    def memory_pair(h, half, logits):
+        for cp in z_copies(h, half):
+            cp.wait_recv()
+        results, _ = finish(2, h, half, [z_in.at[h]], [z_lse_in[h, half]])
+        for k in range(2):
+            head = h * SHARE + 2 * half + k
+            mem_fin[head] = results[k]
+            logits += gate_dot(1, mem_fin, head)
+        return logits
+
+    logits = each_pair(local_pair, jnp.zeros((GROUPS * HEADS_DEV, ROWS), jnp.float32))
+    logits = each_pair(memory_pair, logits)
     lg_out[...] = logits.reshape(GROUPS, HEADS_DEV, ROWS)
 
     def lg(d):
@@ -515,7 +544,7 @@
     for h in range(2):
         for job in range(3):
             for n in range(6):
-                for cp in result_copies(job, h, n):
+                for cp in result_copies(job, h, n, *MESSAGES[n]):
                     cp.wait_send()
         for half in range(2):
             for cp in z_copies(h, half):
@@ -529,14 +558,14 @@
 def on_device(queries, keys, values, mem_keys, mem_values, retrieval, gate_weight, gate_bias):
     bf, f32 = jnp.bfloat16, jnp.float32
     dma = pltpu.SemaphoreType.DMA
-    anywhere = pl.BlockSpec(memory_space=pl.ANY)
+    hbm = pl.BlockSpec(memory_space=pltpu.HBM)
     vmem = pl.BlockSpec(memory_space=pltpu.VMEM)
     part = (SHARE, ROWS, DH)
     stat = (8, ROWS)
     return pl.pallas_call(
         kernel,
         out_shape=jax.ShapeDtypeStruct((ROWS, HEADS_DEV * DH), bf),
-        in_specs=[anywhere] * 5 + [vmem] * 3,
+        in_specs=[hbm] * 8,
         out_specs=vmem,
         scratch_shapes=[
             pltpu.VMEM((2, SIDE, 2) + part, bf),
@@ -558,6 +587,9 @@
             pltpu.VMEM((2 * SHARE, QBLK, DH), f32),
             pltpu.VMEM((GROUPS, HEADS_DEV, ROWS), f32),
             pltpu.VMEM((GROUPS, HEADS_DEV, ROWS), f32),
+            pltpu.VMEM((2, 32), jnp.int32),
+            pltpu.VMEM((2, GROUPS * HEADS_DEV, HEADS_DEV * DH), bf),
+            pltpu.VMEM((1, HEADS_DEV), f32),
             dma((24,)),
             dma((2,)), dma((2,)),
             dma((2, 2, 6)), dma((2, 2, 6)),

time: 104 us -> 101 us (0.971)
  Pallas kernels: 102 us -> 98.6 us
    pallas_call x1, Pallas kernels: 102 us -> 98.6 us  [on_device(): pl.pallas_call(kernel, out_shape=jax.ShapeDtypeStruct((ROWS, HEADS_DEV *...]
where the time goes in v4:
time: 101 us
  Pallas kernels  98.6 us (98%)
  local copies, waits for them, and re-layouts  1.87 us (2%)
    pallas_call x1, Pallas kernels, on_device(): pl.pallas_call(kernel, out_shape=jax.ShapeDtypeStruct((ROWS, HEADS_DEV *...  98.6 us

profile of v4, /device:TPU:1, one launch (start us, length us, event | category | flops | bytes accessed | tf_op | source)
XLA Modules:
  0.0 100.5 jit_solution(1882999093266592766)
XLA Ops:
  0.0 98.6 %shard_map.82 = bf16[256,1024]{1,0:T(8,128)(2,1)} custom-call(bf16[256,1024]{1,0:T(8,128)(2,1)} %q_hbm.1, bf16[256,256]{1,0:T(8,128)(2,1)} %k_hbm.1, bf16[256,256]{1,0:T(8,128)(2,1)} %v_hbm.1, bf16[32,64,256]{2,1,0:T(8,128)(2,1)} %mk_hbm.1, bf16[32,64,256]{2,1,0:T(8,128)(2,1)} %mv_hbm.1, s32[2,32]{1,0:T(2,128)} %bitcast.4, bf16[2,32,1024]{2,1,0:T(8,128)(2,1)} %bitcast.3, ...), custom_call_target="tpu_custom_call" | custom-call | tf_op jit(solution)/shard_map/pallas_call | solution.py:565
  98.7 1.9 %copy.10 = bf16[256,1024]{1,0:T(8,128)(2,1)} copy(bf16[256,1024]{1,0:T(8,128)(2,1)} %shard_map.82) | data formatting | bytes 1048576

commit v5 on v4

--- a/solution.py
+++ b/solution.py
@@ -57,8 +57,8 @@
 
 def kernel(
     q_hbm, k_hbm, v_hbm, mk_hbm, mv_hbm, ids_hbm, gw_hbm, gb_hbm,
-    out_ref,
-    q_buf, kv_buf, mem_buf, tab_buf, tab_sm,
+    out_hbm,
+    out_ref, q_buf, kv_buf, mem_buf, tab_buf, tab_sm,
     part_buf, lse_buf, in_buf, in_lse, z_part, z_lse, z_in, z_lse_in,
     loc_fin, mem_fin, acc_ref, max_ref, lg_out, lg_in, ids_ref, gw_ref, gb_ref,
     l_sem, kvz_s, kvz_r, kva_s, kva_r, qb_s, qb_r, qz_s, qz_r, tab_s, tab_r, ma_s, ma_r,
@@ -279,8 +279,10 @@
     for h in range(2):
         tab_in(h, 2).wait_recv()
         go(tab_z(h, 2, z))
-    on(mem_a_rings, WAIT, 0, 1)
-    on(mem_a_rings, SEND, 4, 5)
+    for n in range(2):
+        for r in mem_a_rings:
+            r[WAIT](n)
+            r[SEND](4 + n)
 
     def local_shard(h, d):
         b = wrap(b_own[h] + d)
@@ -410,8 +412,10 @@
         @pl.when(i == 0)
         def _():
             send_results(0, 0, 1)
-            on(mem_b_rings, WAIT, 0, 1)
-            on(mem_b_rings, SEND, 4, 5)
+            for n in range(2):
+                for r in mem_b_rings:
+                    r[WAIT](n)
+                    r[SEND](4 + n)
 
         pl.when(i == 1)(lambda: send_results(0, 2))
         pl.when(i == 2)(lambda: send_results(0, 3))
@@ -490,10 +494,10 @@
         pl.when(i == 2)(lambda: send_results(1, 3))
         pl.when(i == 3)(lambda: pass_on(1))
         pl.when(i == 4)(lambda: send_results(2, 0, 1))
-        pl.when(i == 4)(lambda: pass_on(0))
         pl.when(i == 5)(lambda: send_results(2, 2))
         pl.when(i == 5)(to_z_peer)
         pl.when(i == 6)(lambda: send_results(2, 3))
+        pl.when(i == 6)(lambda: pass_on(0))
         pl.when(i == 7)(lambda: pass_on(2))
         return carry
 
@@ -535,11 +539,17 @@
     for d in range(1, GROUPS):
         lg(d).wait_recv()
         own = own + lg_in[d]
+    go_out = []
     gate = jax.nn.sigmoid(jnp.transpose(own) + gb_ref[...])
     for head in range(HEADS_DEV):
         share = gate[:, head : head + 1]
         mixed = share * mem_fin[head] + (1.0 - share) * loc_fin[head]
         out_ref[:, head * DH : (head + 1) * DH] = mixed.astype(jnp.bfloat16)
+        if head % 4 == 3:
+            cols = pl.ds((head - 3) * DH, 4 * DH)
+            done = pltpu.make_async_copy(out_ref.at[:, cols], out_hbm.at[:, cols], l_sem.at[head // 4])
+            go_out.append(done)
+            done.start()
 
     for h in range(2):
         for job in range(3):
@@ -553,6 +563,8 @@
         on(rings, SENT, *range(6))
     for cp in started:
         cp.wait_send()
+    for cp in go_out:
+        cp.wait()
 
 
 def on_device(queries, keys, values, mem_keys, mem_values, retrieval, gate_weight, gate_bias):
@@ -566,8 +578,9 @@
         kernel,
         out_shape=jax.ShapeDtypeStruct((ROWS, HEADS_DEV * DH), bf),
         in_specs=[hbm] * 8,
-        out_specs=vmem,
+        out_specs=hbm,
         scratch_shapes=[
+            pltpu.VMEM((ROWS, HEADS_DEV * DH), bf),
             pltpu.VMEM((2, SIDE, 2) + part, bf),
             pltpu.VMEM((2, SIDE, 2, 2, ROWS, DH), bf),
             pltpu.VMEM((2, SIDE, 2, SHARD_BLOCKS, MBLK, DH), bf),

time: 101 us -> 100 us (0.990)
  no operation moved by 1% of the time
where the time goes in v5:
time: 100 us
  Pallas kernels  98.3 us (98%)
  local copies, waits for them, and re-layouts  1.87 us (2%)
    pallas_call x1, Pallas kernels, on_device(): pl.pallas_call(kernel, out_shape=jax.ShapeDtypeStruct((ROWS, HEADS_DEV *...  98.3 us

profile of v5, /device:TPU:1, one launch (start us, length us, event | category | flops | bytes accessed | tf_op | source)
XLA Modules:
  0.0 100.1 jit_solution(11078987183768787949)
XLA Ops:
  0.0 98.3 %shard_map.82 = bf16[256,1024]{1,0:T(8,128)(2,1)} custom-call(bf16[256,1024]{1,0:T(8,128)(2,1)} %q_hbm.1, bf16[256,256]{1,0:T(8,128)(2,1)} %k_hbm.1, bf16[256,256]{1,0:T(8,128)(2,1)} %v_hbm.1, bf16[32,64,256]{2,1,0:T(8,128)(2,1)} %mk_hbm.1, bf16[32,64,256]{2,1,0:T(8,128)(2,1)} %mv_hbm.1, s32[2,32]{1,0:T(2,128)} %bitcast.4, bf16[2,32,1024]{2,1,0:T(8,128)(2,1)} %bitcast.3, ...), custom_call_target="tpu_custom_call" | custom-call | tf_op jit(solution)/shard_map/pallas_call | solution.py:577
  98.3 1.9 %copy.10 = bf16[256,1024]{1,0:T(8,128)(2,1)} copy(bf16[256,1024]{1,0:T(8,128)(2,1)} %shard_map.82) | data formatting | bytes 1048576
